TPU v7x, 32 devices: a whole 2x2x4 slice. The times are simulated.
32 devices in a mesh: ty: 8 (over z, x), tx: 4 (over y, core).
Axes of the slice: x: 2, y: 2, z: 4, core: 2. Of those that a mesh axis runs over, the one named last changes fastest.
Arguments:
- fixed_image: float32 [512, 1024], P('ty', 'tx'), may hold values from -6 to 6
- moving_image: float32 [512, 1024], P('ty', 'tx'), may hold values from -6 to 6
- tissue: int32 [16, 32], P('ty', 'tx'), may hold values from 0 to 1, as said below
Outputs:
- coefficients: float32 [2, 16, 32], P(None, 'ty', 'tx')
- mismatch: float32 [512, 1024], P('ty', 'tx')
Inputs may be any that keep to these rules, and one draw needn't show every extreme that they name: 1 marks a block of 32 x 32 fine pixels that holds tissue, 0 background.
All inputs are finite; a program needn't handle non-finite values.
Results may differ from a plain program's by a relative error of at most 0.0003.
Values sent between devices are 32-bit elements; how exact they have to be, the bound alone decides.
A program may use at most 64 MiB of HBM per device.

v0:
```python
import functools

import jax
import jax.numpy as jnp
from jax import lax
from jax.experimental import pallas as pl
from jax.experimental.pallas import tpu as pltpu
from jax.sharding import PartitionSpec as P

SPACE = 32
REACH_Y = 5
REACH_X = 11
RIM = 16
SEGMENT = 16
SET = 32
OWN_SLOT = 7
MESH = pl.DeviceIdType.MESH
F32 = jnp.float32

half_offsets = ((0, 2), (2, 0), (2, 2), (2, -2), (0, 4), (4, 0))
travels = ((-1, 0), (1, 0), (0, -1), (0, 1), (-1, -1), (-1, 1), (1, -1), (1, 1))


def bspline(values):
    magnitude = jnp.abs(values)
    near_part = 2.0 / 3.0 - magnitude * magnitude + 0.5 * magnitude * magnitude * magnitude
    rest = 2.0 - magnitude
    far_part = rest * rest * rest / 6.0
    return jnp.where(magnitude < 1.0, near_part, jnp.where(magnitude < 2.0, far_part, 0.0))


def moved(values, by_y, by_x):
    rows, lanes = values.shape
    if by_x:
        values = pltpu.roll(values, (-by_x) % lanes, 1)
    if by_y:
        values = pltpu.roll(values, (-by_y) % rows, 0)
    return values


def minds_into(image, lane_step, out_ref):
    total = None
    for index, (offset_y, offset_x) in enumerate(half_offsets):
        gap = image - moved(image, offset_y, lane_step * offset_x)
        square = gap * gap
        rows = square + moved(square, 1, 0) + moved(square, -1, 0)
        box = rows + moved(rows, 0, lane_step) + moved(rows, 0, -lane_step)
        other = moved(box, -offset_y, -lane_step * offset_x)
        out_ref[2 * index, : image.shape[0]] = box
        out_ref[2 * index + 1, : image.shape[0]] = other
        both = box + other
        total = both if total is None else total + both
    return -1.0 / (total / 12.0 + 0.9)


def terms_into(fixed, moving, lane_step, factor, fixed_ref, moving_ref, terms_ref, wide):
    rows = fixed.shape[0]
    height = rows - 16
    fixed_scale = minds_into(fixed, lane_step, fixed_ref)[8 : 8 + height, :wide]
    moving_scale = minds_into(moving, lane_step, moving_ref)
    sums = None
    for index in range(12):
        fixed_mind = jnp.exp(fixed_ref[index, 8 : 8 + height, :wide] * fixed_scale)
        mind = jnp.exp(moving_ref[index, :rows] * moving_scale)
        differ = mind[8 : 8 + height, :wide] - fixed_mind
        slope_y = moved(mind[:, :wide], 1, 0) - moved(mind[:, :wide], -1, 0)
        slope_y = slope_y[8 : 8 + height]
        own = mind[8 : 8 + height]
        slope_x = (moved(own, 0, lane_step) - moved(own, 0, -lane_step))[:, :wide]
        parts = (
            differ * slope_y,
            differ * slope_x,
            slope_y * slope_y,
            slope_y * slope_x,
            slope_x * slope_x,
            differ * differ,
        )
        sums = parts if sums is None else tuple(a + b for a, b in zip(sums, parts))
    once = 1.0 / (2.0 * factor)
    scales = (once, once, once * once, once * once, once * once, 1.0)
    for index in range(6):
        terms_ref[index] = sums[index] * scales[index]


def kernel(
    count_y,
    count_x,
    tissue_hbm,
    fixed_hbm,
    moving_hbm,
    coef_ref,
    mismatch_ref,
    mid,
    left_side,
    right_side,
    full,
    fixed_minds,
    moving_minds,
    fine_terms,
    coarse_terms,
    fine_weight,
    coarse_weight,
    fine_rows,
    coarse_rows,
    fine_cols,
    coarse_cols,
    tissue_ref,
    tiles_box,
    scalar_box,
    load_sem,
    rim_send,
    rim_recv,
    tile_send,
    tile_recv,
    scalar_send,
    scalar_recv,
):
    ty = lax.axis_index("ty")
    tx = lax.axis_index("tx")
    count = count_y * count_x
    me = ty * count_x + tx
    height, breadth = fixed_hbm.shape
    knots = count_x * (breadth // SPACE)
    cells_y, cells_x = height // SPACE, breadth // SPACE

    def peer(step):
        other = lax.rem(me + step, count)
        return (other // count_x, lax.rem(other, count_x))

    def for_peers(act):
        if count <= 64:
            for step in range(1, count):
                act(peer(step))
        else:

            def body(step, carry):
                act(peer(step))
                return carry

            lax.fori_loop(1, count, body, 0)

    tissue_load = pltpu.make_async_copy(tissue_hbm, tissue_ref, load_sem.at[2])
    tissue_load.start()
    loads = []
    for image, ref in enumerate((fixed_hbm, moving_hbm)):
        loads.append(
            pltpu.make_async_copy(ref, mid.at[image, RIM : RIM + height], load_sem.at[image])
        )
        loads[image].start()

    low, high = slice(0, RIM), slice(RIM + height, 2 * RIM + height)

    @pl.when(ty == 0)
    def _():
        for ref in (mid, left_side, right_side):
            ref[:, low] = jnp.zeros((2, RIM, ref.shape[2]), F32)

    @pl.when(ty == count_y - 1)
    def _():
        for ref in (mid, left_side, right_side):
            ref[:, high] = jnp.zeros((2, RIM, ref.shape[2]), F32)

    @pl.when(tx == 0)
    def _():
        left_side[...] = jnp.zeros(left_side.shape, F32)

    @pl.when(tx == count_x - 1)
    def _():
        right_side[...] = jnp.zeros(right_side.shape, F32)

    tiles_box[...] = jnp.zeros(tiles_box.shape, F32)

    barrier = pltpu.get_barrier_semaphore()
    near = 2 <= count_y <= 8 and 2 <= count_x <= 4
    greeted = [(y, x) for y in range(-1, 2) for x in range(-1, 2) if (y, x) != (0, 0)]
    if count_y == 8:
        greeted += [(1 - count_y, 0), (count_y - 1, 0)]

    def here(by_y, by_x):
        to_y, to_x = ty + by_y, tx + by_x
        return (to_y >= 0) & (to_y < count_y) & (to_x >= 0) & (to_x < count_x)

    def greet(device):
        pl.semaphore_signal(barrier, 1, device_id=device, device_id_type=MESH)

    if near:
        for by_y, by_x in greeted:

            @pl.when(here(by_y, by_x))
            def _():
                greet((ty + by_y, tx + by_x))

    else:
        for_peers(greet)

    lane = lax.broadcasted_iota(jnp.int32, (8, breadth), 1)
    for k in range(REACH_X):
        fine_cols[k] = bspline(lane.astype(F32) / SPACE - (k - 1.0))
        coarse_cols[k] = bspline((lane.astype(F32) + 0.5) / SPACE - (k - 1.0))
    row = lax.broadcasted_iota(jnp.int32, (height, 128), 0).astype(F32)
    coarse_row = lax.broadcasted_iota(jnp.int32, (height // 2, 128), 0).astype(F32)
    for r in range(REACH_Y):
        fine_rows[r] = bspline(row / SPACE - (r - 1.0))
        coarse_rows[r] = bspline((2.0 * coarse_row + 0.5) / SPACE - (r - 1.0))
    even = lax.rem(lane, 2) == 0
    tissue_load.wait()
    for i in range(cells_y):
        line = jnp.zeros((8, breadth), F32)
        for j in range(cells_x):
            value = tissue_ref[i, j].astype(F32)
            inside = (lane >= j * SPACE) & (lane < (j + 1) * SPACE)
            line = jnp.where(inside, value, line)
        half = jnp.where(even, line, 0.0)
        for part in range(SPACE // 8):
            start = i * SPACE + part * 8
            fine_weight[start : start + 8] = line
        for part in range(SPACE // 16):
            start = i * (SPACE // 2) + part * 8
            coarse_weight[start : start + 8] = half

    if near:
        edge_y = jnp.where((ty == 0) | (ty == count_y - 1), 1, 0)
        edge_x = jnp.where((tx == 0) | (tx == count_x - 1), 1, 0)
        greeters = (3 - edge_y) * (3 - edge_x) - 1
        if count_y == 8:
            greeters = greeters + edge_y
        pl.semaphore_wait(barrier, greeters)
    else:
        pl.semaphore_wait(barrier, count - 1)

    def rows_of(travel):
        if travel == 0:
            return slice(0, height), slice(RIM, RIM + height)
        if travel > 0:
            return slice(height - RIM, height), low
        return slice(0, RIM), high

    def landing(travel_y, travel_x):
        ref = mid if travel_x == 0 else (left_side if travel_x > 0 else right_side)
        return ref.at[:, rows_of(travel_y)[1]]

    def exists(travel_y, travel_x):
        to_y, to_x = ty + travel_y, tx + travel_x
        return (to_y >= 0) & (to_y < count_y) & (to_x >= 0) & (to_x < count_x)

    for index, (travel_y, travel_x) in enumerate(travels):

        @pl.when(exists(travel_y, travel_x))
        def _():
            source_rows = rows_of(travel_y)[0]
            if travel_x == 0:
                lanes = slice(0, breadth)
            elif travel_x > 0:
                lanes = slice(breadth - 128, breadth)
            else:
                lanes = slice(0, 128)
            for image, ref in enumerate((fixed_hbm, moving_hbm)):
                pltpu.make_async_remote_copy(
                    src_ref=ref.at[source_rows, lanes],
                    dst_ref=landing(travel_y, travel_x).at[image],
                    send_sem=rim_send.at[index],
                    recv_sem=rim_recv.at[index],
                    device_id=(ty + travel_y, tx + travel_x),
                    device_id_type=MESH,
                ).start()

    for load in loads:
        load.wait()

    for index, (travel_y, travel_x) in enumerate(travels):

        @pl.when(exists(-travel_y, -travel_x))
        def _():
            place = landing(travel_y, travel_x)
            pltpu.make_async_copy(place, place, rim_recv.at[index]).wait()

    tiles = breadth // 128
    side_lane = lax.broadcasted_iota(jnp.int32, (height + 2 * RIM, 128), 1)
    for image in range(2):
        for tile in range(tiles):
            full[image * (tiles + 1) + tile] = mid[image, :, tile * 128 : (tile + 1) * 128]
        full[image * (tiles + 1) + tiles] = jnp.where(
            side_lane < 64, right_side[image], left_side[image]
        )

    def fine_image(image):
        base = image * (tiles + 1)
        return jnp.concatenate(
            [full[base + tile, 8 : height + 24] for tile in range(tiles + 1)], axis=1
        )

    def coarse_image(image):
        base = image * (tiles + 1)
        span = height // 2 + RIM
        summed = jnp.concatenate(
            [
                full[base + tile, pl.ds(0, span, stride=2), :]
                + full[base + tile, pl.ds(1, span, stride=2), :]
                for tile in range(tiles + 1)
            ],
            axis=1,
        )
        return 0.25 * (summed + moved(summed, 0, 1))

    terms_into(
        coarse_image(0), coarse_image(1), 2, 2, fixed_minds, moving_minds, coarse_terms, breadth
    )

    small_lane = lax.broadcasted_iota(jnp.int32, (8, 128), 1)
    small_row = lax.broadcasted_iota(jnp.int32, (8, 128), 0)
    knot = lax.rem(small_lane, SEGMENT)
    knot_x = tx * cells_x - 1 + knot
    knot_y = ty * cells_y - 1 + small_row
    valid = (knot < REACH_X) & (small_row < REACH_Y) & (knot_x >= 0) & (knot_x < knots)
    valid = valid & (knot_y >= 0) & (knot_y < count_y * cells_y)
    own = (small_lane < SET) & (knot >= 1) & (knot <= cells_x)
    own = own & (small_row >= 1) & (small_row <= cells_y)

    def displace(window, rows_ref, cols_ref, number=0):
        fields = []
        for member in range(2):
            line = None
            for k in range(REACH_X):
                at = number * SET + member * SEGMENT + k
                part = window[:, at : at + 1] * cols_ref[k]
                line = part if line is None else line + part
            field = None
            for r in range(REACH_Y):
                weights = jnp.concatenate([rows_ref[r]] * tiles, axis=1)
                part = weights * line[r : r + 1, :]
                field = part if field is None else field + part
            fields.append(field)
        return fields

    def gather_up(pixels, rows_ref, cols_ref, number=0):
        out = jnp.zeros((8, 128), F32)
        for member in range(2):
            lines = []
            for r in range(REACH_Y):
                weights = jnp.concatenate([rows_ref[r]] * tiles, axis=1)
                lines.append(jnp.sum(weights * pixels[member], axis=0, keepdims=True))
            lines.append(jnp.zeros((8 - REACH_Y, breadth), F32))
            line = jnp.concatenate(lines, axis=0)
            for k in range(REACH_X):
                column = jnp.sum(line * cols_ref[k], axis=1, keepdims=True)
                at = number * SET + member * SEGMENT + k
                out = jnp.where(small_lane == at, column, out)
        return out

    def slot_of(by_y, by_x):
        return (by_y + 2) * 3 + by_x + 1

    around = [(y, x) for y in range(-2, 3) for x in range(-1, 2) if (y, x) != (0, 0)]

    def send_tile(turn, tile):
        tiles_box[turn, OWN_SLOT] = tile
        for by_y, by_x in around:

            @pl.when(exists(by_y, by_x))
            def _():
                slot = slot_of(-by_y, -by_x)
                pltpu.make_async_remote_copy(
                    src_ref=tiles_box.at[turn, OWN_SLOT],
                    dst_ref=tiles_box.at[turn, slot],
                    send_sem=tile_send.at[slot],
                    recv_sem=tile_recv.at[turn, slot],
                    device_id=(ty + by_y, tx + by_x),
                    device_id_type=MESH,
                ).start()

    def collect_tiles(turn):
        for by_y, by_x in around:

            @pl.when(exists(by_y, by_x))
            def _():
                slot = slot_of(by_y, by_x)
                place = tiles_box.at[turn, slot]
                pltpu.make_async_copy(place, place, tile_recv.at[turn, slot]).wait()

        window = None
        for by_x in range(-1, 2):
            total = None
            for by_y in range(-2, 3):
                part = tiles_box[turn, slot_of(by_y, by_x)]
                if by_y:
                    part = pltpu.roll(part, (2 * by_y) % 8, 0)
                if by_y == 2:
                    part = jnp.where(small_row >= 4, part, 0.0)
                if by_y == -2:
                    part = jnp.where(small_row < 1, part, 0.0)
                total = part if total is None else total + part
            if by_x:
                total = pltpu.roll(total, (8 * by_x) % 128, 1)
                reached = (knot >= 8) if by_x > 0 else (knot < REACH_X - 8)
                total = jnp.where(reached, total, 0.0)
            window = total if window is None else window + total
        return jnp.where(valid, window, 0.0)

    def send_scalars(turn, row):
        scalar_box[turn, me] = row

        def act(device):
            pltpu.make_async_remote_copy(
                src_ref=scalar_box.at[turn, me],
                dst_ref=scalar_box.at[turn, me],
                send_sem=scalar_send.at[turn],
                recv_sem=scalar_recv.at[turn],
                device_id=device,
                device_id_type=MESH,
            ).start()

        for_peers(act)

    def collect_scalars(turn):
        part = scalar_box.at[turn, 0 : count - 1]
        pltpu.make_async_copy(part, part, scalar_recv.at[turn]).wait()
        row = jnp.sum(scalar_box[turn], axis=0)
        lanes = lax.broadcasted_iota(jnp.int32, (1, 128), 1)
        return [
            jnp.sum(
                jnp.where((lanes >= SET * i) & (lanes < SET * (i + 1)), row, 0.0), keepdims=True
            )
            for i in range(4)
        ]

    def scalars(first, second, dense):
        third = jnp.where(own, second * second, 0.0)
        middle = jnp.where(own, first * second, 0.0)
        lead = jnp.where(own, first * first, 0.0)
        packed = lead + pltpu.roll(middle, SET, 1) + pltpu.roll(third, 2 * SET, 1)
        row = jnp.sum(packed, axis=0, keepdims=True)
        dense = dense + pltpu.roll(dense, 64, 1)
        dense = dense + pltpu.roll(dense, 32, 1)
        lanes = lax.broadcasted_iota(jnp.int32, (1, 128), 1)
        return jnp.where(lanes >= 3 * SET, dense, row)

    def pulled(terms_ref, motion):
        return (
            terms_ref[2] * motion[0] + terms_ref[3] * motion[1],
            terms_ref[3] * motion[0] + terms_ref[4] * motion[1],
        )

    def weighted(weight_ref, pair):
        return [weight_ref[...] * pair[0], weight_ref[...] * pair[1]]

    def density_row(weight_ref, motion, pull):
        dense = weight_ref[...] * (motion[0] * pull[0] + motion[1] * pull[1])
        line = jnp.sum(dense, axis=0, keepdims=True)
        total = line[:, :128]
        for tile in range(1, tiles):
            total = total + line[:, tile * 128 : (tile + 1) * 128]
        return total

    def steps_of(first, middle, third, fourth):
        step = first / middle
        norm = first - 2.0 * step * middle + step * step * third
        curvature = middle - 2.0 * step * third + step * step * fourth
        return step, norm / curvature

    send_tile(
        0,
        gather_up(
            weighted(coarse_weight, (coarse_terms[0], coarse_terms[1])), coarse_rows, coarse_cols
        ),
    )
    terms_into(fine_image(0), fine_image(1), 1, 1, fixed_minds, moving_minds, fine_terms, breadth)
    fine_start = gather_up(
        weighted(fine_weight, (fine_terms[0], fine_terms[1])), fine_rows, fine_cols, 1
    )
    gradient0 = collect_tiles(0)

    motion = displace(gradient0, coarse_rows, coarse_cols)
    part = gather_up(
        weighted(coarse_weight, pulled(coarse_terms, motion)), coarse_rows, coarse_cols
    )
    send_tile(1, part + fine_start)
    fine_motion0 = displace(gradient0, fine_rows, fine_cols)
    fine_part0 = gather_up(
        weighted(fine_weight, pulled(fine_terms, fine_motion0)), fine_rows, fine_cols
    )
    gradient1 = collect_tiles(1)

    motion = displace(gradient1, coarse_rows, coarse_cols)
    dense = density_row(coarse_weight, motion, pulled(coarse_terms, motion))
    send_scalars(0, scalars(gradient0, gradient1, dense))
    fine_motion1 = displace(gradient1, fine_rows, fine_cols)
    fine_part1 = gather_up(
        weighted(fine_weight, pulled(fine_terms, fine_motion1)), fine_rows, fine_cols, 1
    )
    send_tile(2, fine_part0 + fine_part1)
    fine_gradient = pltpu.roll(gradient1, 128 - SET, 1)
    images = collect_tiles(2)
    step0, step1 = steps_of(*collect_scalars(0))
    near, far = -(step0 + step1), step0 * step1
    control = near * gradient0 + far * gradient1
    direction = fine_gradient + near * images + far * pltpu.roll(images, 128 - SET, 1)

    motion2 = displace(direction, fine_rows, fine_cols)
    send_tile(
        3,
        gather_up(weighted(fine_weight, pulled(fine_terms, motion2)), fine_rows, fine_cols),
    )
    field_y = near * fine_motion0[0] + far * fine_motion1[0]
    field_x = near * fine_motion0[1] + far * fine_motion1[1]
    image = collect_tiles(3)

    motion3 = displace(image, fine_rows, fine_cols)
    dense = density_row(fine_weight, motion3, pulled(fine_terms, motion3))
    send_scalars(1, scalars(direction, image, dense))
    step0, step1 = steps_of(*collect_scalars(1))
    near, far = -(step0 + step1), step0 * step1
    control = control + near * direction + far * image
    field_y = field_y + near * motion2[0] + far * motion3[0]
    field_x = field_x + near * motion2[1] + far * motion3[1]
    pull_y, pull_x = pulled(fine_terms, (field_y, field_x))
    mismatch_ref[...] = (
        fine_terms[5]
        + 2.0 * (fine_terms[0] * field_y + fine_terms[1] * field_x)
        + field_y * pull_y
        + field_x * pull_x
    )
    for member in range(2):
        start = member * SEGMENT + 1
        coef_ref[member] = control[1 : 1 + cells_y, start : start + cells_x]

    for index, (travel_y, travel_x) in enumerate(travels):

        @pl.when(exists(travel_y, travel_x))
        def _():
            place = landing(travel_y, travel_x)
            pltpu.make_async_copy(place, place, rim_send.at[index]).wait()

    for by_y, by_x in around:

        @pl.when(exists(by_y, by_x))
        def _():
            slot = slot_of(-by_y, -by_x)
            place = tiles_box.at[:, slot]
            pltpu.make_async_copy(place, place, tile_send.at[slot]).wait()

    for turn in range(2):
        part = scalar_box.at[turn, 0 : count - 1]
        pltpu.make_async_copy(part, part, scalar_send.at[turn]).wait()


def shards(count_y, count_x, fixed_image, moving_image, tissue):
    height, breadth = fixed_image.shape
    cells_y, cells_x = height // SPACE, breadth // SPACE
    count = count_y * count_x
    tall, full_lanes = height + 2 * RIM, breadth + 128
    vmem = pltpu.VMEM
    scratch = [
        vmem((2, tall, breadth), F32),
        vmem((2, tall, 128), F32),
        vmem((2, tall, 128), F32),
        vmem((2 * (breadth // 128 + 1), tall, 128), F32),
        vmem((12, height + 16, full_lanes), F32),
        vmem((12, height + 16, full_lanes), F32),
        vmem((6, height, breadth), F32),
        vmem((6, height // 2, breadth), F32),
        vmem((height, breadth), F32),
        vmem((height // 2, breadth), F32),
        vmem((REACH_Y, height, 128), F32),
        vmem((REACH_Y, height // 2, 128), F32),
        vmem((REACH_X, 8, breadth), F32),
        vmem((REACH_X, 8, breadth), F32),
        pltpu.SMEM((cells_y, cells_x), jnp.int32),
        vmem((4, 15, 8, 128), F32),
        vmem((2, count, 1, 128), F32),
        pltpu.SemaphoreType.DMA((3,)),
        pltpu.SemaphoreType.DMA((8,)),
        pltpu.SemaphoreType.DMA((8,)),
        pltpu.SemaphoreType.DMA((15,)),
        pltpu.SemaphoreType.DMA((4, 15)),
        pltpu.SemaphoreType.DMA((2,)),
        pltpu.SemaphoreType.DMA((2,)),
    ]
    return pl.pallas_call(
        functools.partial(kernel, count_y, count_x),
        out_shape=(
            jax.ShapeDtypeStruct((2, cells_y, cells_x), F32),
            jax.ShapeDtypeStruct((height, breadth), F32),
        ),
        in_specs=[
            pl.BlockSpec(memory_space=pltpu.HBM),
            pl.BlockSpec(memory_space=pltpu.HBM),
            pl.BlockSpec(memory_space=pltpu.HBM),
        ],
        out_specs=(
            pl.BlockSpec(memory_space=pltpu.VMEM),
            pl.BlockSpec(memory_space=pltpu.VMEM),
        ),
        scratch_shapes=scratch,
        compiler_params=pltpu.CompilerParams(
            collective_id=0, has_side_effects=True, vmem_limit_bytes=63 * 1024 * 1024
        ),
    )(tissue, fixed_image, moving_image)


def solution(mesh):
    placed = (P("ty", "tx"), P("ty", "tx"), P("ty", "tx"))
    return jax.shard_map(
        functools.partial(shards, mesh.shape["ty"], mesh.shape["tx"]),
        mesh=mesh,
        in_specs=placed,
        out_specs=(P(None, "ty", "tx"), P("ty", "tx")),
        check_vma=False,
    )
```

profile of v0, /device:TPU:0, one launch (start us, length us, event | category | flops | bytes accessed | tf_op | source)
XLA Modules:
  0.0 36.7 jit_solution(12551659439493304230)
XLA Ops:
  0.6 33.3 %shard_map.50 = (f32[2,2,8]{2,1,0:T(2,128)}, f32[64,256]{1,0:T(8,128)}) custom-call(s32[2,8]{1,0:T(2,128)} %tissue_hbm.1, f32[64,256]{1,0:T(8,128)} %fixed_hbm.1, f32[64,256]{1,0:T(8,128)} %moving_hbm.1), custom_call_target="tpu_custom_call" | custom-call | tf_op jit(solution)/shard_map/pallas_call | solution.py:578
  33.9 0.0 copy-start
  33.9 0.7 %copy-done = f32[2,2,8]{2,1,0:T(2,128)S(1)} copy-done((f32[2,2,8]{2,1,0:T(2,128)S(1)}, f32[2,2,8]{2,1,0:T(2,128)}, u32[]{:S(2)}) %copy-start) | copy-done | bytes 152
  34.6 0.6 %copy.7 = f32[2,2,8]{2,1,0:T(2,128)} copy(f32[2,2,8]{2,1,0:T(2,128)S(1)} %copy-done) | data formatting | bytes 256
  35.2 1.5 %copy.8 = f32[64,256]{1,0:T(8,128)} copy(f32[64,256]{1,0:T(8,128)} %get-tuple-element.5) | data formatting | bytes 131072
Async XLA Ops:
  33.9 0.7 %copy-start = (f32[2,2,8]{2,1,0:T(2,128)S(1)}, f32[2,2,8]{2,1,0:T(2,128)}, u32[]{:S(2)}) copy-start(f32[2,2,8]{2,1,0:T(2,128)} %get-tuple-element.4) | copy-start | bytes 388
where the time goes:
time: 36.9 us; the launch traced here: 36.7 us
  Pallas kernels  33.3 us (90%)
  local copies, waits for them, and re-layouts  2.73 us (7%)
  between operations  0.65 us (2%)
    pallas_call x1, Pallas kernels, shards(): pl.pallas_call(functools.partial(kernel, count_y, count_x), out_shape=(ja...  33.3 us
    unnamed x4, local copies, waits for them, and re-layouts  2.73 us

commit v1 on v0

--- a/solution.py
+++ b/solution.py
@@ -543,7 +543,7 @@
         pltpu.make_async_copy(part, part, scalar_send.at[turn]).wait()
 
 
-def shards(count_y, count_x, fixed_image, moving_image, tissue):
+def registered(count_y, count_x, tissue, fixed_image, moving_image):
     height, breadth = fixed_image.shape
     cells_y, cells_x = height // SPACE, breadth // SPACE
     count = count_y * count_x
@@ -592,9 +592,36 @@
         ),
         scratch_shapes=scratch,
         compiler_params=pltpu.CompilerParams(
-            collective_id=0, has_side_effects=True, vmem_limit_bytes=63 * 1024 * 1024
+            collective_id=0, has_side_effects=True, vmem_limit_bytes=16 * 1024 * 1024
         ),
     )(tissue, fixed_image, moving_image)
+
+
+def closing(coef_in, mismatch_in, coef_out, mismatch_out, sem):
+    loads = [
+        pltpu.make_async_copy(mismatch_in, mismatch_out, sem.at[0]),
+        pltpu.make_async_copy(coef_in, coef_out, sem.at[1]),
+    ]
+    for load in loads:
+        load.start()
+    for load in loads:
+        load.wait()
+
+
+def shards(count_y, count_x, fixed_image, moving_image, tissue):
+    held = [pltpu.with_memory_space_constraint(x, pltpu.HBM) for x in (tissue, fixed_image, moving_image)]
+    coef, mismatch = registered(count_y, count_x, *held)
+    return pl.pallas_call(
+        closing,
+        out_shape=(
+            jax.ShapeDtypeStruct(coef.shape, F32),
+            jax.ShapeDtypeStruct(mismatch.shape, F32),
+        ),
+        in_specs=[pl.BlockSpec(memory_space=pl.ANY)] * 2,
+        out_specs=(pl.BlockSpec(memory_space=pltpu.HBM),) * 2,
+        scratch_shapes=[pltpu.SemaphoreType.DMA((2,))],
+        compiler_params=pltpu.CompilerParams(vmem_limit_bytes=4 * 1024 * 1024),
+    )(coef, mismatch)
 
 
 def solution(mesh):

time: 36.9 us -> 34.1 us (0.924)
  local copies, waits for them, and re-layouts: 2.73 us -> 0 us
    unnamed x4 -> x0, local copies, waits for them, and re-layouts: 2.73 us -> none
    pallas_call x1 -> x2, Pallas kernels: 33.3 us -> 33.3 us  [the longest x1 32.7 us: registered(): pl.pallas_call(functools.partial(kernel, count_y, count_x), out_shape=(ja...]
where the time goes in v1:
time: 34.1 us; the launch traced here: 34 us
  Pallas kernels  33.3 us (98%)
  between operations  0.64 us (2%)
    pallas_call x1, Pallas kernels, registered(): pl.pallas_call(functools.partial(kernel, count_y, count_x), out_shape=(ja...  32.7 us

profile of v1, /device:TPU:0, one launch (start us, length us, event | category | flops | bytes accessed | tf_op | source)
XLA Modules:
  0.0 34.0 jit_solution(7561155072060798501)
XLA Ops:
  0.6 32.7 %shard_map.50 = (f32[2,2,8]{2,1,0:T(2,128)S(1)}, f32[64,256]{1,0:T(8,128)S(1)}) custom-call(s32[2,8]{1,0:T(2,128)} %tissue_hbm.1, f32[64,256]{1,0:T(8,128)} %fixed_hbm.1, f32[64,256]{1,0:T(8,128)} %moving_hbm.1), custom_call_target="tpu_custom_call" | custom-call | tf_op jit(solution)/shard_map/pallas_call | solution.py:578
  33.3 0.7 %shard_map.51 = (f32[2,2,8]{2,1,0:T(2,128)}, f32[64,256]{1,0:T(8,128)}) custom-call(f32[2,2,8]{2,1,0:T(2,128)S(1)} %get-tuple-element.4.coef_in, f32[64,256]{1,0:T(8,128)S(1)} %get-tuple-element.5.mismatch_in), custom_call_target="tpu_custom_call" | custom-call | tf_op jit(solution)/shard_map/pallas_call | solution.py:614

commit v2 on v1

--- a/solution.py
+++ b/solution.py
@@ -2,6 +2,7 @@
 
 import jax
 import jax.numpy as jnp
+import numpy as np
 from jax import lax
 from jax.experimental import pallas as pl
 from jax.experimental.pallas import tpu as pltpu
@@ -16,6 +17,9 @@
 OWN_SLOT = 7
 MESH = pl.DeviceIdType.MESH
 F32 = jnp.float32
+B16 = jnp.bfloat16
+BLOCK = 16
+LARGEST = 64
 
 half_offsets = ((0, 2), (2, 0), (2, 2), (2, -2), (0, 4), (4, 0))
 travels = ((-1, 0), (1, 0), (0, -1), (0, 1), (-1, -1), (-1, 1), (1, -1), (1, 1))
@@ -82,7 +86,7 @@
         terms_ref[index] = sums[index] * scales[index]
 
 
-def kernel(
+def spread_kernel(
     count_y,
     count_x,
     tissue_hbm,
@@ -543,7 +547,472 @@
         pltpu.make_async_copy(part, part, scalar_send.at[turn]).wait()
 
 
-def registered(count_y, count_x, tissue, fixed_image, moving_image):
+def window_pairs(span):
+    return [(k, k + d) for d in range(4) for k in range(span - d)]
+
+
+def split(values):
+    high = values.astype(B16)
+    return high, (values - high.astype(F32)).astype(B16)
+
+
+def spline_array(values):
+    magnitude = np.abs(values)
+    rest = 2.0 - magnitude
+    near_part = 2.0 / 3.0 - magnitude**2 + 0.5 * magnitude**3
+    far_part = rest**3 / 6.0
+    return np.where(magnitude < 1.0, near_part, np.where(magnitude < 2.0, far_part, 0.0))
+
+
+def split_array(values):
+    values = values.astype(np.float32)
+    high = values.astype(B16)
+    return high, (values - high.astype(np.float32)).astype(B16)
+
+
+def level_tables(height, breadth, factor):
+    row_at = factor * np.arange(height // factor) + (factor - 1) / 2.0
+    col_at = np.arange(breadth) + (factor - 1) / 2.0
+    rows = spline_array(row_at[None, :] / SPACE - (np.arange(REACH_Y)[:, None] - 1.0))
+    cols = spline_array(col_at[:, None] / SPACE - (np.arange(REACH_X)[None, :] - 1.0))
+    row_pairs = np.zeros((BLOCK, row_at.size))
+    for at, (r, other) in enumerate(window_pairs(REACH_Y)):
+        row_pairs[at] = rows[r] * rows[other]
+    lines = np.zeros((2, BLOCK, row_at.size))
+    for member in range(2):
+        lines[member, member * REACH_Y : (member + 1) * REACH_Y] = rows
+    pairs = window_pairs(REACH_X)
+    col_table = np.zeros((4, breadth, 128))
+    for comp in range(3):
+        for at, (k, other) in enumerate(pairs):
+            col_table[comp, :, comp * len(pairs) + at] = cols[:, k] * cols[:, other]
+    col_table[3, :, 3 * len(pairs) : 3 * len(pairs) + REACH_X] = cols
+
+    def left(table):
+        high, low = split_array(table)
+        return np.concatenate([high, high, low], axis=1)
+
+    high, low = split_array(col_table.reshape(4 * breadth, 128))
+    return (
+        left(row_pairs),
+        np.concatenate([left(lines[0]), left(lines[1])], axis=1),
+        np.concatenate([high, low], axis=1),
+    )
+
+
+def assembly_tables(count_y, count_x, cells_y, cells_x):
+    knots_y, knots_x = count_y * cells_y, count_x * cells_x
+    pairs = window_pairs(REACH_X)
+    width = 8 * knots_x
+    cols = np.zeros((count_x * 128, 3 * width + 128), np.float32)
+    for tx in range(count_x):
+        for comp in range(3):
+            for at, (k, other) in enumerate(pairs):
+                first, second = tx * cells_x - 1 + k, tx * cells_x - 1 + other
+                if first < 0 or second >= knots_x:
+                    continue
+                source, gap = tx * 128 + comp * len(pairs) + at, other - k
+                cols[source, comp * width + (3 + gap) * knots_x + first] = 1.0
+                cols[source, comp * width + (3 - gap) * knots_x + second] = 1.0
+        for k in range(REACH_X):
+            knot = tx * cells_x - 1 + k
+            if 0 <= knot < knots_x:
+                for group in range(128 // knots_x):
+                    cols[tx * 128 + 3 * len(pairs) + k, 3 * width + group * knots_x + knot] = 1.0
+    rows = np.zeros((9 * knots_y, count_y * BLOCK), np.float32)
+    for ty in range(count_y):
+        for at, (r, other) in enumerate(window_pairs(REACH_Y)):
+            first, second = ty * cells_y - 1 + r, ty * cells_y - 1 + other
+            if first < 0 or second >= knots_y:
+                continue
+            rows[(3 + other - r) * knots_y + first, ty * BLOCK + at] = 1.0
+            rows[(3 - other + r) * knots_y + second, ty * BLOCK + at] = 1.0
+        for member in range(2):
+            for r in range(REACH_Y):
+                knot = ty * cells_y - 1 + r
+                if 0 <= knot < knots_y:
+                    rows[(7 + member) * knots_y + knot, ty * BLOCK + member * REACH_Y + r] = 1.0
+    return cols.astype(B16), np.concatenate([rows, rows], axis=1).astype(B16)
+
+
+def dot(left, right):
+    return jnp.dot(left, right, preferred_element_type=F32)
+
+
+def gathered_kernel(
+    count_y,
+    count_x,
+    tissue_hbm,
+    fixed_hbm,
+    moving_hbm,
+    *rest,
+):
+    tables_hbm, rest = rest[:8], rest[8:]
+    coef_ref, mismatch_ref = rest[:2]
+    tables, rest = rest[2:10], rest[10:]
+    (
+        mid,
+        left_side,
+        right_side,
+        full,
+        fixed_minds,
+        moving_minds,
+        fine_terms,
+        coarse_terms,
+        fine_weight,
+        coarse_weight,
+        tissue_ref,
+        boxes,
+        stencils,
+        last_rows,
+        last_cols,
+        load_sem,
+        table_sem,
+        rim_send,
+        rim_recv,
+        block_send,
+        block_recv,
+        relay_send,
+        relay_recv,
+    ) = rest
+    fine_tables, coarse_tables, (gather_cols, gather_rows) = tables[:3], tables[3:6], tables[6:]
+    ty = lax.axis_index("ty")
+    tx = lax.axis_index("tx")
+    count = count_y * count_x
+    half = count // 2
+    me = ty * count_x + tx
+    parity = lax.rem(tx, 2)
+    place = ty * (count_x // 2) + tx // 2
+    sibling = (ty, tx + 1 - 2 * parity)
+    height, breadth = fixed_hbm.shape
+    cells_y, cells_x = height // SPACE, breadth // SPACE
+    knots_y, knots_x = count_y * cells_y, count_x * cells_x
+    width = 8 * knots_x
+
+    def exists(by_y, by_x):
+        to_y, to_x = ty + by_y, tx + by_x
+        return (to_y >= 0) & (to_y < count_y) & (to_x >= 0) & (to_x < count_x)
+
+    barrier = pltpu.get_barrier_semaphore()
+    for step in range(1, count):
+        other = lax.rem(me + step, count)
+        pl.semaphore_signal(
+            barrier,
+            1,
+            device_id=(other // count_x, lax.rem(other, count_x)),
+            device_id_type=MESH,
+        )
+
+    tissue_load = pltpu.make_async_copy(tissue_hbm, tissue_ref, load_sem.at[2])
+    tissue_load.start()
+    loads = []
+    for image, ref in enumerate((fixed_hbm, moving_hbm)):
+        loads.append(
+            pltpu.make_async_copy(ref, mid.at[image, RIM : RIM + height], load_sem.at[image])
+        )
+        loads[image].start()
+    table_loads = []
+    for index, (source, target) in enumerate(zip(tables_hbm, tables)):
+        table_loads.append(pltpu.make_async_copy(source, target, table_sem.at[index]))
+        table_loads[index].start()
+
+    low, high = slice(0, RIM), slice(RIM + height, 2 * RIM + height)
+
+    @pl.when(ty == 0)
+    def _():
+        for ref in (mid, left_side, right_side):
+            ref[:, low] = jnp.zeros((2, RIM, ref.shape[2]), F32)
+
+    @pl.when(ty == count_y - 1)
+    def _():
+        for ref in (mid, left_side, right_side):
+            ref[:, high] = jnp.zeros((2, RIM, ref.shape[2]), F32)
+
+    @pl.when(tx == 0)
+    def _():
+        left_side[...] = jnp.zeros(left_side.shape, F32)
+
+    @pl.when(tx == count_x - 1)
+    def _():
+        right_side[...] = jnp.zeros(right_side.shape, F32)
+
+    lane = lax.broadcasted_iota(jnp.int32, (8, breadth), 1)
+    even = lax.rem(lane, 2) == 0
+    tissue_load.wait()
+    for i in range(cells_y):
+        line = jnp.zeros((8, breadth), F32)
+        for j in range(cells_x):
+            value = tissue_ref[i, j].astype(F32)
+            inside = (lane >= j * SPACE) & (lane < (j + 1) * SPACE)
+            line = jnp.where(inside, value, line)
+        halved = jnp.where(even, line, 0.0)
+        for part in range(SPACE // 8):
+            start = i * SPACE + part * 8
+            fine_weight[start : start + 8] = line
+        for part in range(SPACE // 16):
+            start = i * (SPACE // 2) + part * 8
+            coarse_weight[start : start + 8] = halved
+
+    def rows_of(travel):
+        if travel == 0:
+            return slice(0, height), slice(RIM, RIM + height)
+        if travel > 0:
+            return slice(height - RIM, height), low
+        return slice(0, RIM), high
+
+    def landing(travel_y, travel_x):
+        ref = mid if travel_x == 0 else (left_side if travel_x > 0 else right_side)
+        return ref.at[:, rows_of(travel_y)[1]]
+
+    pl.semaphore_wait(barrier, count - 1)
+
+    for index, (travel_y, travel_x) in enumerate(travels):
+
+        @pl.when(exists(travel_y, travel_x))
+        def _():
+            source_rows = rows_of(travel_y)[0]
+            if travel_x == 0:
+                lanes = slice(0, breadth)
+            elif travel_x > 0:
+                lanes = slice(breadth - 128, breadth)
+            else:
+                lanes = slice(0, 128)
+            for image, ref in enumerate((fixed_hbm, moving_hbm)):
+                pltpu.make_async_remote_copy(
+                    src_ref=ref.at[source_rows, lanes],
+                    dst_ref=landing(travel_y, travel_x).at[image],
+                    send_sem=rim_send.at[index],
+                    recv_sem=rim_recv.at[index],
+                    device_id=(ty + travel_y, tx + travel_x),
+                    device_id_type=MESH,
+                ).start()
+
+    knot = lax.broadcasted_iota(jnp.int32, (128, breadth), 0)
+    at_x = lax.broadcasted_iota(jnp.int32, (128, breadth), 1).astype(F32) / SPACE
+    last = bspline(at_x - (knot - tx * cells_x).astype(F32))
+    last_high, last_low = split(jnp.where(knot < knots_x, last, 0.0))
+    last_cols[:, :breadth] = last_high
+    last_cols[:, breadth:] = last_low
+    knot = lax.broadcasted_iota(jnp.int32, (height, 128), 1)
+    at_y = lax.broadcasted_iota(jnp.int32, (height, 128), 0).astype(F32) / SPACE
+    third = knot // knots_y
+    last_high, last_low = split(
+        bspline(at_y - (lax.rem(knot, knots_y) - ty * cells_y).astype(F32))
+    )
+    kept = jnp.where(third < 2, last_high.astype(F32), last_low.astype(F32))
+    last_rows[...] = jnp.where(third < 3, kept, 0.0).astype(B16)
+
+    for load in loads:
+        load.wait()
+
+    for index, (travel_y, travel_x) in enumerate(travels):
+
+        @pl.when(exists(-travel_y, -travel_x))
+        def _():
+            spot = landing(travel_y, travel_x)
+            pltpu.make_async_copy(spot, spot, rim_recv.at[index]).wait()
+
+    tiles = breadth // 128
+    side_lane = lax.broadcasted_iota(jnp.int32, (height + 2 * RIM, 128), 1)
+    for image in range(2):
+        for tile in range(tiles):
+            full[image * (tiles + 1) + tile] = mid[image, :, tile * 128 : (tile + 1) * 128]
+        full[image * (tiles + 1) + tiles] = jnp.where(
+            side_lane < 64, right_side[image], left_side[image]
+        )
+
+    def fine_image(image):
+        base = image * (tiles + 1)
+        return jnp.concatenate(
+            [full[base + tile, 8 : height + 24] for tile in range(tiles + 1)], axis=1
+        )
+
+    def coarse_image(image):
+        base = image * (tiles + 1)
+        span = height // 2 + RIM
+        summed = jnp.concatenate(
+            [
+                full[base + tile, pl.ds(0, span, stride=2), :]
+                + full[base + tile, pl.ds(1, span, stride=2), :]
+                for tile in range(tiles + 1)
+            ],
+            axis=1,
+        )
+        return 0.25 * (summed + moved(summed, 0, 1))
+
+    def block_of(terms_ref, weight_ref, level):
+        row_pairs, row_lines, col_table = level
+        weight = weight_ref[...]
+        upper, lower = split(
+            jnp.concatenate([weight * terms_ref[index] for index in (2, 3, 4)], axis=1)
+        )
+        pairs = dot(row_pairs[...], jnp.concatenate([upper, lower, upper], axis=0))
+        stack = []
+        for member in range(2):
+            upper, lower = split(weight * terms_ref[member])
+            stack += [upper, lower, upper]
+        lines = dot(row_lines[...], jnp.concatenate(stack, axis=0))
+        upper, lower = split(jnp.concatenate([pairs, lines], axis=1))
+        out = dot(jnp.concatenate([upper, lower], axis=0), col_table[...])
+        return out[:BLOCK, :128] + out[BLOCK:, :128] + out[:BLOCK, 128:]
+
+    def send_block(level, block):
+        boxes[level, parity, place] = block
+        for step_y in range(count_y):
+            for step_x in range(count_x // 2):
+                if step_y + step_x == 0:
+                    continue
+                to_y = lax.rem(ty + step_y, count_y)
+                to_x = 2 * lax.rem(tx // 2 + step_x, count_x // 2) + parity
+                pltpu.make_async_remote_copy(
+                    src_ref=boxes.at[level, parity, place],
+                    dst_ref=boxes.at[level, parity, place],
+                    send_sem=block_send.at[level],
+                    recv_sem=block_recv.at[level],
+                    device_id=(to_y, to_x),
+                    device_id_type=MESH,
+                ).start()
+
+    def relay_of(level):
+        return pltpu.make_async_remote_copy(
+            src_ref=boxes.at[level, parity],
+            dst_ref=boxes.at[level, parity],
+            send_sem=relay_send.at[level],
+            recv_sem=relay_recv.at[level],
+            device_id=sibling,
+            device_id_type=MESH,
+        )
+
+    def relay(level):
+        part = boxes.at[level, 0, 0 : half - 1]
+        pltpu.make_async_copy(part, part, block_recv.at[level]).wait()
+        relay_of(level).start()
+        spot = boxes.at[level, 1 - parity]
+        pltpu.make_async_copy(spot, spot, relay_recv.at[level]).wait()
+
+    def assemble(level):
+        columns = []
+        for to_x in range(count_x):
+            columns.append(
+                jnp.concatenate(
+                    [
+                        boxes[level, to_x % 2, to_y * (count_x // 2) + to_x // 2]
+                        for to_y in range(count_y)
+                    ],
+                    axis=0,
+                )
+            )
+        upper, lower = split(jnp.concatenate(columns, axis=1))
+        out = dot(jnp.concatenate([upper, lower], axis=0), gather_cols[...])
+        rows = count_y * BLOCK
+        upper, lower = split(out[:rows] + out[rows:])
+        stencils[level] = dot(gather_rows[...], jnp.concatenate([upper, lower], axis=0))
+
+    group = lax.broadcasted_iota(jnp.int32, (knots_y, 128), 1) // knots_x
+
+    def spread(values):
+        halves = []
+        for start in (-3, 1):
+            out = None
+            for index in range(4):
+                gap = start + index
+                rolled = pltpu.roll(values, (-gap) % 128, 1) if gap else values
+                out = rolled if out is None else jnp.where(group >= index, rolled, out)
+            halves.append(out)
+        return halves
+
+    def start_of(level):
+        return [
+            stencils[level, (7 + member) * knots_y : (8 + member) * knots_y, 3 * width :]
+            for member in range(2)
+        ]
+
+    def pull(level, pair):
+        spreads = [spread(values) for values in pair]
+        sums = [None, None]
+        for gap in range(-3, 4):
+            at = (gap + 3) * knots_y
+            for source in range(2):
+                for part in range(2):
+                    shifted = spreads[source][part]
+                    if gap:
+                        shifted = pltpu.roll(shifted, (-gap) % knots_y, 0)
+                    for member in range(2):
+                        lanes = (member + source) * width + part * 128
+                        term = stencils[level, at : at + knots_y, lanes : lanes + 128] * shifted
+                        old = sums[member]
+                        sums[member] = term if old is None else old + term
+        out = []
+        for total in sums:
+            total = total + pltpu.roll(total, 64, 1)
+            out.append(total + pltpu.roll(total, 32, 1))
+        return out
+
+    def inner(first, second):
+        return jnp.sum(first[0] * second[0] + first[1] * second[1], keepdims=True)
+
+    def descend(level, control, gradient):
+        image = pull(level, gradient)
+        step = inner(gradient, gradient) / inner(gradient, image)
+        control = [c - step * g for c, g in zip(control, gradient)]
+        gradient = [g - step * i for g, i in zip(gradient, image)]
+        image = pull(level, gradient)
+        step = inner(gradient, gradient) / inner(gradient, image)
+        return [c - step * g for c, g in zip(control, gradient)]
+
+    for load in table_loads:
+        load.wait()
+    terms_into(
+        coarse_image(0), coarse_image(1), 2, 2, fixed_minds, moving_minds, coarse_terms, breadth
+    )
+    send_block(0, block_of(coarse_terms, coarse_weight, coarse_tables))
+    terms_into(fine_image(0), fine_image(1), 1, 1, fixed_minds, moving_minds, fine_terms, breadth)
+    send_block(1, block_of(fine_terms, fine_weight, fine_tables))
+
+    relay(0)
+    assemble(0)
+    control = [jnp.zeros((knots_y, 128), F32)] * 2
+    control = descend(0, control, start_of(0))
+    relay(1)
+    assemble(1)
+    gradient = [b + i for b, i in zip(start_of(1), pull(1, control))]
+    control = descend(1, control, gradient)
+
+    upper, lower = split(jnp.concatenate(control, axis=0))
+    rows = 2 * knots_y
+    out = dot(jnp.concatenate([upper, lower], axis=0), last_cols[...])
+    lines = out[:rows, :breadth] + out[rows:, :breadth] + out[:rows, breadth:]
+    upper, lower = split(jnp.concatenate([lines[:knots_y], lines[knots_y:]], axis=1))
+    blank = jnp.zeros((128 - 3 * knots_y, 2 * breadth), B16)
+    field = dot(last_rows[...], jnp.concatenate([upper, lower, upper, blank], axis=0))
+    field_y, field_x = field[:, :breadth], field[:, breadth:]
+    pull_y = fine_terms[2] * field_y + fine_terms[3] * field_x
+    pull_x = fine_terms[3] * field_y + fine_terms[4] * field_x
+    mismatch_ref[...] = (
+        fine_terms[5]
+        + 2.0 * (fine_terms[0] * field_y + fine_terms[1] * field_x)
+        + field_y * pull_y
+        + field_x * pull_x
+    )
+    for member in range(2):
+        own = pltpu.roll(control[member], lax.rem(128 - cells_x * tx, 128), 1)
+        own = pltpu.roll(own, lax.rem(knots_y - cells_y * ty, knots_y), 0)
+        coef_ref[member] = own[:cells_y, :cells_x]
+
+    for index, (travel_y, travel_x) in enumerate(travels):
+
+        @pl.when(exists(travel_y, travel_x))
+        def _():
+            spot = landing(travel_y, travel_x)
+            pltpu.make_async_copy(spot, spot, rim_send.at[index]).wait()
+
+    for level in range(2):
+        part = boxes.at[level, 0, 0 : half - 1]
+        pltpu.make_async_copy(part, part, block_send.at[level]).wait()
+        relay_of(level).wait_send()
+
+
+def spread_call(count_y, count_x, tissue, fixed_image, moving_image):
     height, breadth = fixed_image.shape
     cells_y, cells_x = height // SPACE, breadth // SPACE
     count = count_y * count_x
@@ -576,7 +1045,7 @@
         pltpu.SemaphoreType.DMA((2,)),
     ]
     return pl.pallas_call(
-        functools.partial(kernel, count_y, count_x),
+        functools.partial(spread_kernel, count_y, count_x),
         out_shape=(
             jax.ShapeDtypeStruct((2, cells_y, cells_x), F32),
             jax.ShapeDtypeStruct((height, breadth), F32),
@@ -608,9 +1077,70 @@
         load.wait()
 
 
+def gathered_call(count_y, count_x, tissue, fixed_image, moving_image):
+    height, breadth = fixed_image.shape
+    cells_y, cells_x = height // SPACE, breadth // SPACE
+    count = count_y * count_x
+    tall, full_lanes = height + 2 * RIM, breadth + 128
+    vmem, dma = pltpu.VMEM, pltpu.SemaphoreType.DMA
+    tables = (
+        level_tables(height, breadth, 1)
+        + level_tables(height, breadth, 2)
+        + assembly_tables(count_y, count_x, cells_y, cells_x)
+    )
+    scratch = [vmem(table.shape, B16) for table in tables] + [
+        vmem((2, tall, breadth), F32),
+        vmem((2, tall, 128), F32),
+        vmem((2, tall, 128), F32),
+        vmem((2 * (breadth // 128 + 1), tall, 128), F32),
+        vmem((12, height + 16, full_lanes), F32),
+        vmem((12, height + 16, full_lanes), F32),
+        vmem((6, height, breadth), F32),
+        vmem((6, height // 2, breadth), F32),
+        vmem((height, breadth), F32),
+        vmem((height // 2, breadth), F32),
+        pltpu.SMEM((cells_y, cells_x), jnp.int32),
+        vmem((2, 2, count // 2, BLOCK, 128), F32),
+        vmem((2, tables[7].shape[0], tables[6].shape[1]), F32),
+        vmem((height, 128), B16),
+        vmem((128, 2 * breadth), B16),
+        dma((3,)),
+        dma((8,)),
+        dma((8,)),
+        dma((8,)),
+        dma((2,)),
+        dma((2,)),
+        dma((2,)),
+        dma((2,)),
+    ]
+    held = [
+        pltpu.with_memory_space_constraint(jnp.asarray(table), pltpu.HBM) for table in tables
+    ]
+    return pl.pallas_call(
+        functools.partial(gathered_kernel, count_y, count_x),
+        out_shape=(
+            jax.ShapeDtypeStruct((2, cells_y, cells_x), F32),
+            jax.ShapeDtypeStruct((height, breadth), F32),
+        ),
+        in_specs=[pl.BlockSpec(memory_space=pltpu.HBM)] * 11,
+        out_specs=(
+            pl.BlockSpec(memory_space=pltpu.VMEM),
+            pl.BlockSpec(memory_space=pltpu.VMEM),
+        ),
+        scratch_shapes=scratch,
+        compiler_params=pltpu.CompilerParams(
+            collective_id=1, has_side_effects=True, vmem_limit_bytes=32 * 1024 * 1024
+        ),
+    )(tissue, fixed_image, moving_image, *held)
+
+
 def shards(count_y, count_x, fixed_image, moving_image, tissue):
     held = [pltpu.with_memory_space_constraint(x, pltpu.HBM) for x in (tissue, fixed_image, moving_image)]
-    coef, mismatch = registered(count_y, count_x, *held)
+    height, breadth = fixed_image.shape
+    fits = height == 2 * SPACE and breadth == 8 * SPACE and count_x % 2 == 0
+    fits = fits and count_x * (breadth // SPACE) == 32 and count_y * count_x <= LARGEST
+    call = gathered_call if fits else spread_call
+    coef, mismatch = call(count_y, count_x, *held)
     return pl.pallas_call(
         closing,
         out_shape=(

time: 34.1 us -> 26.2 us (0.77)
  the two profiles are of different devices: /device:TPU:0 before, /device:TPU:1 now
where the time goes in v2:
time: 26.2 us; the launch traced here: 26.1 us
  Pallas kernels  25.4 us (97%)
  between operations  0.64 us (2%)
    pallas_call x1, Pallas kernels, gathered_call(): pl.pallas_call(functools.partial(gathered_kernel, count_y, count_x), out_...  24.8 us
    pallas_call x1, Pallas kernels, shards(): pl.pallas_call(closing, out_shape=(jax.ShapeDtypeStruct(coef.shape, F32),...  0.65 us

profile of v2, /device:TPU:1, one launch (start us, length us, event | category | flops | bytes accessed | tf_op | source)
XLA Modules:
  0.0 26.1 jit_solution(593526469405742485)
XLA Ops:
  0.6 24.8 %shard_map.122 = (f32[2,2,8]{2,1,0:T(2,128)S(1)}, f32[64,256]{1,0:T(8,128)S(1)}) custom-call(s32[2,8]{1,0:T(2,128)} %tissue_hbm.1, f32[64,256]{1,0:T(8,128)} %fixed_hbm.1, f32[64,256]{1,0:T(8,128)} %moving_hbm.1, bf16[16,192]{1,0:T(8,128)(2,1)} %constant.16.clone.rest_0_, bf16[16,384]{1,0:T(8,128)(2,1)} %constant.17.clone.rest_1_, ...), custom_call_target="tpu_custom_call" | custom-call | tf_op jit(solution)/shard_map/pallas_call | solution.py:1119
  25.4 0.7 %shard_map.123 = (f32[2,2,8]{2,1,0:T(2,128)}, f32[64,256]{1,0:T(8,128)}) custom-call(f32[2,2,8]{2,1,0:T(2,128)S(1)} %get-tuple-element.4.coef_in, f32[64,256]{1,0:T(8,128)S(1)} %get-tuple-element.5.mismatch_in), custom_call_target="tpu_custom_call" | custom-call | tf_op jit(solution)/shard_map/pallas_call | solution.py:1144

commit v3 on v2

--- a/solution.py
+++ b/solution.py
@@ -22,6 +22,7 @@
 LARGEST = 64
 
 half_offsets = ((0, 2), (2, 0), (2, 2), (2, -2), (0, 4), (4, 0))
+far_greets = (2, -2, 4)
 travels = ((-1, 0), (1, 0), (0, -1), (0, 1), (-1, -1), (-1, 1), (1, -1), (1, 1))
 
 
@@ -572,7 +573,7 @@
 
 def level_tables(height, breadth, factor):
     row_at = factor * np.arange(height // factor) + (factor - 1) / 2.0
-    col_at = np.arange(breadth) + (factor - 1) / 2.0
+    col_at = np.arange(breadth) - (factor - 1) / 2.0
     rows = spline_array(row_at[None, :] / SPACE - (np.arange(REACH_Y)[:, None] - 1.0))
     cols = spline_array(col_at[:, None] / SPACE - (np.arange(REACH_X)[None, :] - 1.0))
     row_pairs = np.zeros((BLOCK, row_at.size))
@@ -639,6 +640,82 @@
     return jnp.dot(left, right, preferred_element_type=F32)
 
 
+def shifted_tiles(parts, step, wanted):
+    lane = lax.broadcasted_iota(jnp.int32, parts[0].shape, 1)
+    rolled = [pltpu.roll(part, (-step) % 128, 1) for part in parts]
+    count = len(parts)
+    out = []
+    for at in range(wanted):
+        if step > 0:
+            out.append(jnp.where(lane < 128 - step, rolled[at], rolled[(at + 1) % count]))
+        else:
+            out.append(jnp.where(lane >= -step, rolled[at], rolled[(at - 1) % count]))
+    return out
+
+
+def minds_tiled(scale, boxes_ref, minds_ref, rows):
+    count = scale.shape[1] // 128
+    for index in range(12):
+        mind = jnp.exp(boxes_ref[index, :rows] * scale)
+        for tile in range(count):
+            minds_ref[index, tile, :rows] = mind[:, tile * 128 : (tile + 1) * 128]
+
+
+def sums_into(minds_ref, fixed_of, lane_step, factor, terms_ref):
+    height, breadth = terms_ref.shape[1:]
+    tiles = breadth // 128
+    once = 1.0 / (2.0 * factor)
+    scales = (once, once, once * once, once * once, once * once, 1.0)
+    for start in range(0, height, 8):
+        base = 8 + start
+        sums = None
+        for index in range(12):
+            own = [minds_ref[index, tile, base : base + 8] for tile in range(tiles + 1)]
+            fixed = fixed_of(index, base, own)
+            ahead = shifted_tiles(own, lane_step, tiles)
+            behind = shifted_tiles(own, -lane_step, tiles)
+            parts = []
+            for tile in range(tiles):
+                differ = own[tile] - fixed[tile]
+                slope_y = (
+                    minds_ref[index, tile, base + 1 : base + 9]
+                    - minds_ref[index, tile, base - 1 : base + 7]
+                )
+                slope_x = ahead[tile] - behind[tile]
+                parts += [
+                    differ * slope_y,
+                    differ * slope_x,
+                    slope_y * slope_y,
+                    slope_y * slope_x,
+                    slope_x * slope_x,
+                    differ * differ,
+                ]
+            sums = parts if sums is None else [a + b for a, b in zip(sums, parts)]
+        for tile in range(tiles):
+            for term in range(6):
+                terms_ref[term, start : start + 8, tile * 128 : (tile + 1) * 128] = (
+                    sums[6 * tile + term] * scales[term]
+                )
+
+
+def greeted_by(count_y, count_x, y, x):
+    near = {(y + by_y, x + by_x) for by_y, by_x in travels}
+    near = {(a, b) for a, b in near if 0 <= a < count_y and 0 <= b < count_x}
+    return near | {((y + step) % count_y, x ^ 1) for step in far_greets}
+
+
+def two_steps_reach(count_y, count_x):
+    if count_y < 8 or count_x % 2:
+        return False
+    every = [(y, x) for y in range(count_y) for x in range(count_x)]
+    greeted = {at: greeted_by(count_y, count_x, *at) for at in every}
+    for y, x in every:
+        known = greeted[y, x].union(*(greeted[at] for at in greeted[y, x]))
+        if not {at for at in every if (at[1] - x) % 2 == 0 and at != (y, x)} <= known:
+            return False
+    return True
+
+
 def gathered_kernel(
     count_y,
     count_x,
@@ -655,8 +732,10 @@
         left_side,
         right_side,
         full,
+        fixed_boxes,
+        boxes_ref,
+        minds_ref,
         fixed_minds,
-        moving_minds,
         fine_terms,
         coarse_terms,
         fine_weight,
@@ -674,6 +753,7 @@
         block_recv,
         relay_send,
         relay_recv,
+        ready,
     ) = rest
     fine_tables, coarse_tables, (gather_cols, gather_rows) = tables[:3], tables[3:6], tables[6:]
     ty = lax.axis_index("ty")
@@ -693,15 +773,33 @@
         to_y, to_x = ty + by_y, tx + by_x
         return (to_y >= 0) & (to_y < count_y) & (to_x >= 0) & (to_x < count_x)
 
+    few = two_steps_reach(count_y, count_x)
+
+    def greet_far(semaphore):
+        for step in far_greets:
+            other = (lax.rem(ty + step + count_y, count_y), sibling[1])
+            pl.semaphore_signal(semaphore, 1, device_id=other, device_id_type=MESH)
+
     barrier = pltpu.get_barrier_semaphore()
-    for step in range(1, count):
-        other = lax.rem(me + step, count)
-        pl.semaphore_signal(
-            barrier,
-            1,
-            device_id=(other // count_x, lax.rem(other, count_x)),
-            device_id_type=MESH,
-        )
+    if few:
+        for by_y, by_x in travels:
+
+            @pl.when(exists(by_y, by_x))
+            def _():
+                pl.semaphore_signal(
+                    barrier, 1, device_id=(ty + by_y, tx + by_x), device_id_type=MESH
+                )
+
+        greet_far(barrier)
+        edge_y = jnp.where((ty == 0) | (ty == count_y - 1), 1, 0)
+        edge_x = jnp.where((tx == 0) | (tx == count_x - 1), 1, 0)
+        greeters = (3 - edge_y) * (3 - edge_x) - 1 + len(far_greets)
+    else:
+        for step in range(1, count):
+            other = lax.rem(me + step, count)
+            other = (other // count_x, lax.rem(other, count_x))
+            pl.semaphore_signal(barrier, 1, device_id=other, device_id_type=MESH)
+        greeters = count - 1
 
     tissue_load = pltpu.make_async_copy(tissue_hbm, tissue_ref, load_sem.at[2])
     tissue_load.start()
@@ -745,7 +843,7 @@
             value = tissue_ref[i, j].astype(F32)
             inside = (lane >= j * SPACE) & (lane < (j + 1) * SPACE)
             line = jnp.where(inside, value, line)
-        halved = jnp.where(even, line, 0.0)
+        halved = jnp.where(even, 0.0, line)
         for part in range(SPACE // 8):
             start = i * SPACE + part * 8
             fine_weight[start : start + 8] = line
@@ -764,7 +862,7 @@
         ref = mid if travel_x == 0 else (left_side if travel_x > 0 else right_side)
         return ref.at[:, rows_of(travel_y)[1]]
 
-    pl.semaphore_wait(barrier, count - 1)
+    pl.semaphore_wait(barrier, greeters)
 
     for index, (travel_y, travel_x) in enumerate(travels):
 
@@ -787,6 +885,9 @@
                     device_id_type=MESH,
                 ).start()
 
+    if few:
+        greet_far(ready)
+
     knot = lax.broadcasted_iota(jnp.int32, (128, breadth), 0)
     at_x = lax.broadcasted_iota(jnp.int32, (128, breadth), 1).astype(F32) / SPACE
     last = bspline(at_x - (knot - tx * cells_x).astype(F32))
@@ -827,18 +928,52 @@
             [full[base + tile, 8 : height + 24] for tile in range(tiles + 1)], axis=1
         )
 
-    def coarse_image(image):
-        base = image * (tiles + 1)
+    def coarse_pair():
         span = height // 2 + RIM
-        summed = jnp.concatenate(
-            [
-                full[base + tile, pl.ds(0, span, stride=2), :]
-                + full[base + tile, pl.ds(1, span, stride=2), :]
-                for tile in range(tiles + 1)
-            ],
-            axis=1,
+        summed = []
+        for image in range(2):
+            base = image * (tiles + 1)
+            summed.append(
+                jnp.concatenate(
+                    [
+                        full[base + tile, pl.ds(0, span, stride=2), :]
+                        + full[base + tile, pl.ds(1, span, stride=2), :]
+                        for tile in range(tiles + 1)
+                    ],
+                    axis=1,
+                )
+            )
+        fixed, moving = summed
+        at = lax.broadcasted_iota(jnp.int32, fixed.shape, 1)
+        pair = jnp.where(
+            lax.rem(at, 2) == 0, fixed + moved(fixed, 0, 1), moving + moved(moving, 0, -1)
         )
-        return 0.25 * (summed + moved(summed, 0, 1))
+        return 0.25 * pair
+
+    def coarse_terms_into():
+        pair = coarse_pair()
+        minds_tiled(minds_into(pair, 2, boxes_ref), boxes_ref, minds_ref, pair.shape[0])
+
+        def fixed_of(index, base, own):
+            return shifted_tiles(own, -1, tiles)
+
+        sums_into(minds_ref, fixed_of, 2, 2, coarse_terms)
+
+    def fine_terms_into():
+        fixed_minds[...] = minds_into(fine_image(0), 1, fixed_boxes)[8 : 8 + height, :breadth]
+        image = fine_image(1)
+        minds_tiled(minds_into(image, 1, boxes_ref), boxes_ref, minds_ref, image.shape[0])
+
+        def fixed_of(index, base, own):
+            return [
+                jnp.exp(
+                    fixed_boxes[index, base : base + 8, tile * 128 : (tile + 1) * 128]
+                    * fixed_minds[base - 8 : base, tile * 128 : (tile + 1) * 128]
+                )
+                for tile in range(tiles)
+            ]
+
+        sums_into(minds_ref, fixed_of, 1, 1, fine_terms)
 
     def block_of(terms_ref, weight_ref, level):
         row_pairs, row_lines, col_table = level
@@ -858,10 +993,9 @@
 
     def send_block(level, block):
         boxes[level, parity, place] = block
-        for step_y in range(count_y):
-            for step_x in range(count_x // 2):
-                if step_y + step_x == 0:
-                    continue
+        order = [(a, b) for a in range(count_y) for b in range(count_x // 2) if a + b]
+        for step_y, step_x in sorted(order, key=lambda p: abs(p[0] - count_y // 2) - p[1]):
+            if True:
                 to_y = lax.rem(ty + step_y, count_y)
                 to_x = 2 * lax.rem(tx // 2 + step_x, count_x // 2) + parity
                 pltpu.make_async_remote_copy(
@@ -962,11 +1096,12 @@
 
     for load in table_loads:
         load.wait()
-    terms_into(
-        coarse_image(0), coarse_image(1), 2, 2, fixed_minds, moving_minds, coarse_terms, breadth
-    )
-    send_block(0, block_of(coarse_terms, coarse_weight, coarse_tables))
-    terms_into(fine_image(0), fine_image(1), 1, 1, fixed_minds, moving_minds, fine_terms, breadth)
+    coarse_terms_into()
+    coarse_block = block_of(coarse_terms, coarse_weight, coarse_tables)
+    if few:
+        pl.semaphore_wait(ready, len(far_greets))
+    send_block(0, coarse_block)
+    fine_terms_into()
     send_block(1, block_of(fine_terms, fine_weight, fine_tables))
 
     relay(0)
@@ -1095,6 +1230,8 @@
         vmem((2 * (breadth // 128 + 1), tall, 128), F32),
         vmem((12, height + 16, full_lanes), F32),
         vmem((12, height + 16, full_lanes), F32),
+        vmem((12, breadth // 128 + 1, height + 16, 128), F32),
+        vmem((height, breadth), F32),
         vmem((6, height, breadth), F32),
         vmem((6, height // 2, breadth), F32),
         vmem((height, breadth), F32),
@@ -1112,6 +1249,7 @@
         dma((2,)),
         dma((2,)),
         dma((2,)),
+        pltpu.SemaphoreType.REGULAR,
     ]
     held = [
         pltpu.with_memory_space_constraint(jnp.asarray(table), pltpu.HBM) for table in tables

time: 26.2 us -> 24.3 us (0.927)
  Pallas kernels: 25.4 us -> 23.6 us
    pallas_call x1, Pallas kernels: 24.8 us -> 22.9 us  [gathered_call(): pl.pallas_call(functools.partial(gathered_kernel, count_y, count_x), out_...]
where the time goes in v3:
time: 24.3 us; the launch traced here: 24.2 us
  Pallas kernels  23.6 us (97%)
  between operations  0.64 us (3%)
    pallas_call x1, Pallas kernels, gathered_call(): pl.pallas_call(functools.partial(gathered_kernel, count_y, count_x), out_...  22.9 us
    pallas_call x1, Pallas kernels, shards(): pl.pallas_call(closing, out_shape=(jax.ShapeDtypeStruct(coef.shape, F32),...  0.65 us

profile of v3, /device:TPU:1, one launch (start us, length us, event | category | flops | bytes accessed | tf_op | source)
XLA Modules:
  0.0 24.2 jit_solution(8336636885537521886)
XLA Ops:
  0.6 22.9 %shard_map.122 = (f32[2,2,8]{2,1,0:T(2,128)S(1)}, f32[64,256]{1,0:T(8,128)S(1)}) custom-call(s32[2,8]{1,0:T(2,128)} %tissue_hbm.1, f32[64,256]{1,0:T(8,128)} %fixed_hbm.1, f32[64,256]{1,0:T(8,128)} %moving_hbm.1, bf16[16,192]{1,0:T(8,128)(2,1)} %constant.16.clone.rest_0_, bf16[16,384]{1,0:T(8,128)(2,1)} %constant.17.clone.rest_1_, ...), custom_call_target="tpu_custom_call" | custom-call | tf_op jit(solution)/shard_map/pallas_call | solution.py:1257
  23.5 0.7 %shard_map.123 = (f32[2,2,8]{2,1,0:T(2,128)}, f32[64,256]{1,0:T(8,128)}) custom-call(f32[2,2,8]{2,1,0:T(2,128)S(1)} %get-tuple-element.4.coef_in, f32[64,256]{1,0:T(8,128)S(1)} %get-tuple-element.5.mismatch_in), custom_call_target="tpu_custom_call" | custom-call | tf_op jit(solution)/shard_map/pallas_call | solution.py:1282

commit v4 on v3

--- a/solution.py
+++ b/solution.py
@@ -19,6 +19,8 @@
 F32 = jnp.float32
 B16 = jnp.bfloat16
 BLOCK = 16
+PARTS = 3
+LOG2E = 1.4426950408889634
 LARGEST = 64
 
 half_offsets = ((0, 2), (2, 0), (2, 2), (2, -2), (0, 4), (4, 0))
@@ -571,11 +573,41 @@
     return high, (values - high.astype(np.float32)).astype(B16)
 
 
+def strided_columns(breadth, factor):
+    lane, part = np.arange(128)[None, :], np.arange(PARTS)[:, None]
+    if factor == 1:
+        column = PARTS * lane + part - 8
+        return column, (column >= 0) & (column < breadth)
+    column = PARTS * (lane - 64) + part - 6
+    return column, (lane >= 64) & (column >= 0) & (column < breadth // 2)
+
+
+def natural_lane(column, breadth):
+    return column if column >= 0 else breadth + 128 + column
+
+
+def stride_tables(breadth):
+    size = breadth + 128
+    fine = np.zeros((size, PARTS * 128))
+    for place in range(breadth + 16):
+        fine[natural_lane(place - 8, breadth), place % PARTS * 128 + place // PARTS] = 1.0
+    coarse = np.zeros((2, size, PARTS * 128))
+    for image in range(2):
+        for place in range(breadth // 2 + 12):
+            at = place % PARTS * 128 + image * 64 + place // PARTS
+            for side in range(2):
+                coarse[image, natural_lane(2 * (place - 6) + side, breadth), at] = 0.25
+    back = fine[:breadth].T
+    return tuple(table.astype(B16) for table in (fine, coarse[0], coarse[1], back))
+
+
 def level_tables(height, breadth, factor):
     row_at = factor * np.arange(height // factor) + (factor - 1) / 2.0
-    col_at = np.arange(breadth) - (factor - 1) / 2.0
+    column, taken = strided_columns(breadth, factor)
+    col_at = (factor * column + (factor - 1) / 2.0).reshape(-1)
     rows = spline_array(row_at[None, :] / SPACE - (np.arange(REACH_Y)[:, None] - 1.0))
     cols = spline_array(col_at[:, None] / SPACE - (np.arange(REACH_X)[None, :] - 1.0))
+    cols = cols * taken.reshape(-1, 1)
     row_pairs = np.zeros((BLOCK, row_at.size))
     for at, (r, other) in enumerate(window_pairs(REACH_Y)):
         row_pairs[at] = rows[r] * rows[other]
@@ -583,7 +615,7 @@
     for member in range(2):
         lines[member, member * REACH_Y : (member + 1) * REACH_Y] = rows
     pairs = window_pairs(REACH_X)
-    col_table = np.zeros((4, breadth, 128))
+    col_table = np.zeros((4, col_at.size, 128))
     for comp in range(3):
         for at, (k, other) in enumerate(pairs):
             col_table[comp, :, comp * len(pairs) + at] = cols[:, k] * cols[:, other]
@@ -593,7 +625,7 @@
         high, low = split_array(table)
         return np.concatenate([high, high, low], axis=1)
 
-    high, low = split_array(col_table.reshape(4 * breadth, 128))
+    high, low = split_array(col_table.reshape(4 * col_at.size, 128))
     return (
         left(row_pairs),
         np.concatenate([left(lines[0]), left(lines[1])], axis=1),
@@ -607,19 +639,20 @@
     width = 8 * knots_x
     cols = np.zeros((count_x * 128, 3 * width + 128), np.float32)
     for tx in range(count_x):
+        start = (tx % 2 * (count_x // 2) + tx // 2) * 128
         for comp in range(3):
             for at, (k, other) in enumerate(pairs):
                 first, second = tx * cells_x - 1 + k, tx * cells_x - 1 + other
                 if first < 0 or second >= knots_x:
                     continue
-                source, gap = tx * 128 + comp * len(pairs) + at, other - k
+                source, gap = start + comp * len(pairs) + at, other - k
                 cols[source, comp * width + (3 + gap) * knots_x + first] = 1.0
                 cols[source, comp * width + (3 - gap) * knots_x + second] = 1.0
         for k in range(REACH_X):
             knot = tx * cells_x - 1 + k
             if 0 <= knot < knots_x:
                 for group in range(128 // knots_x):
-                    cols[tx * 128 + 3 * len(pairs) + k, 3 * width + group * knots_x + knot] = 1.0
+                    cols[start + 3 * len(pairs) + k, 3 * width + group * knots_x + knot] = 1.0
     rows = np.zeros((9 * knots_y, count_y * BLOCK), np.float32)
     for ty in range(count_y):
         for at, (r, other) in enumerate(window_pairs(REACH_Y)):
@@ -640,48 +673,73 @@
     return jnp.dot(left, right, preferred_element_type=F32)
 
 
-def shifted_tiles(parts, step, wanted):
-    lane = lax.broadcasted_iota(jnp.int32, parts[0].shape, 1)
-    rolled = [pltpu.roll(part, (-step) % 128, 1) for part in parts]
-    count = len(parts)
+def strided(parts, step):
     out = []
-    for at in range(wanted):
-        if step > 0:
-            out.append(jnp.where(lane < 128 - step, rolled[at], rolled[(at + 1) % count]))
-        else:
-            out.append(jnp.where(lane >= -step, rolled[at], rolled[(at - 1) % count]))
+    for at in range(PARTS):
+        carry, source = divmod(at + step, PARTS)
+        part = parts[source]
+        out.append(pltpu.roll(part, (-carry) % 128, 1) if carry else part)
     return out
 
 
-def minds_tiled(scale, boxes_ref, minds_ref, rows):
-    count = scale.shape[1] // 128
+def lowered(parts, step):
+    return [pltpu.roll(part, (-step) % part.shape[0], 0) for part in parts] if step else parts
+
+
+def split_three(values):
+    high = values.astype(B16)
+    rest = values - high.astype(F32)
+    middle = rest.astype(B16)
+    return [high, middle, (rest - middle.astype(F32)).astype(B16)]
+
+
+def boxes_into(parts, boxes_ref):
+    rows = parts[0].shape[0]
+    turned = {step: strided(parts, step) for step in (2, -2, 4)}
+    turned[0] = parts
+    total = None
+    for index, (offset_y, offset_x) in enumerate(half_offsets):
+        other = lowered(turned[offset_x], offset_y)
+        square = [(p - q) * (p - q) for p, q in zip(parts, other)]
+        lines = [
+            p + q + r for p, q, r in zip(square, lowered(square, 1), lowered(square, -1))
+        ]
+        box = [p + q + r for p, q, r in zip(lines, strided(lines, 1), strided(lines, -1))]
+        back = lowered(strided(box, -offset_x) if offset_x else box, -offset_y)
+        for at in range(PARTS):
+            boxes_ref[2 * index, at, :rows] = box[at]
+            boxes_ref[2 * index + 1, at, :rows] = back[at]
+        both = [p + q for p, q in zip(box, back)]
+        total = both if total is None else [p + q for p, q in zip(total, both)]
+    return [-LOG2E / (part / 12.0 + 0.9) for part in total]
+
+
+def minds_tiled(scale, boxes_ref, minds_ref):
+    rows = scale[0].shape[0]
     for index in range(12):
-        mind = jnp.exp(boxes_ref[index, :rows] * scale)
-        for tile in range(count):
-            minds_ref[index, tile, :rows] = mind[:, tile * 128 : (tile + 1) * 128]
-
-
-def sums_into(minds_ref, fixed_of, lane_step, factor, terms_ref):
-    height, breadth = terms_ref.shape[1:]
-    tiles = breadth // 128
+        for at in range(PARTS):
+            minds_ref[index, at, :rows] = jnp.exp2(boxes_ref[index, at, :rows] * scale[at])
+
+
+def sums_into(minds_ref, fixed_of, factor, terms_ref):
+    height = terms_ref.shape[1]
     once = 1.0 / (2.0 * factor)
     scales = (once, once, once * once, once * once, once * once, 1.0)
     for start in range(0, height, 8):
         base = 8 + start
         sums = None
         for index in range(12):
-            own = [minds_ref[index, tile, base : base + 8] for tile in range(tiles + 1)]
+            own = [minds_ref[index, at, base : base + 8] for at in range(PARTS)]
             fixed = fixed_of(index, base, own)
-            ahead = shifted_tiles(own, lane_step, tiles)
-            behind = shifted_tiles(own, -lane_step, tiles)
+            ahead, behind = strided(own, 1), strided(own, -1)
             parts = []
-            for tile in range(tiles):
-                differ = own[tile] - fixed[tile]
+            for at in range(PARTS):
+                differ = own[at] - fixed[at]
                 slope_y = (
-                    minds_ref[index, tile, base + 1 : base + 9]
-                    - minds_ref[index, tile, base - 1 : base + 7]
+                    minds_ref[index, at, base + 1 : base + 9]
+                    - minds_ref[index, at, base - 1 : base + 7]
                 )
-                slope_x = ahead[tile] - behind[tile]
+                slope_x = ahead[at] - behind[at]
                 parts += [
                     differ * slope_y,
                     differ * slope_x,
@@ -691,10 +749,10 @@
                     differ * differ,
                 ]
             sums = parts if sums is None else [a + b for a, b in zip(sums, parts)]
-        for tile in range(tiles):
+        for at in range(PARTS):
             for term in range(6):
-                terms_ref[term, start : start + 8, tile * 128 : (tile + 1) * 128] = (
-                    sums[6 * tile + term] * scales[term]
+                terms_ref[term, start : start + 8, at * 128 : (at + 1) * 128] = (
+                    sums[6 * at + term] * scales[term]
                 )
 
 
@@ -724,9 +782,9 @@
     moving_hbm,
     *rest,
 ):
-    tables_hbm, rest = rest[:8], rest[8:]
+    tables_hbm, rest = rest[:12], rest[12:]
     coef_ref, mismatch_ref = rest[:2]
-    tables, rest = rest[2:10], rest[10:]
+    tables, rest = rest[2:14], rest[14:]
     (
         mid,
         left_side,
@@ -755,7 +813,8 @@
         relay_recv,
         ready,
     ) = rest
-    fine_tables, coarse_tables, (gather_cols, gather_rows) = tables[:3], tables[3:6], tables[6:]
+    fine_tables, coarse_tables, (gather_cols, gather_rows) = tables[:3], tables[3:6], tables[6:8]
+    fine_stride, fixed_stride, moving_stride, stride_back = tables[8:]
     ty = lax.axis_index("ty")
     tx = lax.axis_index("tx")
     count = count_y * count_x
@@ -768,6 +827,8 @@
     cells_y, cells_x = height // SPACE, breadth // SPACE
     knots_y, knots_x = count_y * cells_y, count_x * cells_x
     width = 8 * knots_x
+    used = len(window_pairs(REACH_Y))
+    wide = PARTS * 128
 
     def exists(by_y, by_x):
         to_y, to_x = ty + by_y, tx + by_x
@@ -809,11 +870,8 @@
             pltpu.make_async_copy(ref, mid.at[image, RIM : RIM + height], load_sem.at[image])
         )
         loads[image].start()
-    table_loads = []
-    for index, (source, target) in enumerate(zip(tables_hbm, tables)):
-        table_loads.append(pltpu.make_async_copy(source, target, table_sem.at[index]))
-        table_loads[index].start()
-
+
+    boxes[:, :, :, used:] = jnp.zeros((2, 2, half, BLOCK - used, 128), F32)
     low, high = slice(0, RIM), slice(RIM + height, 2 * RIM + height)
 
     @pl.when(ty == 0)
@@ -834,22 +892,28 @@
     def _():
         right_side[...] = jnp.zeros(right_side.shape, F32)
 
-    lane = lax.broadcasted_iota(jnp.int32, (8, breadth), 1)
-    even = lax.rem(lane, 2) == 0
+    lane = lax.broadcasted_iota(jnp.int32, (8, 128), 1)
     tissue_load.wait()
     for i in range(cells_y):
-        line = jnp.zeros((8, breadth), F32)
-        for j in range(cells_x):
-            value = tissue_ref[i, j].astype(F32)
-            inside = (lane >= j * SPACE) & (lane < (j + 1) * SPACE)
-            line = jnp.where(inside, value, line)
-        halved = jnp.where(even, 0.0, line)
-        for part in range(SPACE // 8):
-            start = i * SPACE + part * 8
-            fine_weight[start : start + 8] = line
-        for part in range(SPACE // 16):
-            start = i * (SPACE // 2) + part * 8
-            coarse_weight[start : start + 8] = halved
+        for at in range(PARTS):
+            fine_at = PARTS * lane + at - 8
+            coarse_at = jnp.where(lane < 64, -1, 2 * (PARTS * (lane - 64) + at - 6))
+            fine_line = jnp.zeros((8, 128), F32)
+            coarse_line = jnp.zeros((8, 128), F32)
+            for j in range(cells_x):
+                value = tissue_ref[i, j].astype(F32)
+                low_x, high_x = j * SPACE, (j + 1) * SPACE
+                inside = (fine_at >= low_x) & (fine_at < high_x)
+                fine_line = jnp.where(inside, value, fine_line)
+                inside = (coarse_at >= low_x) & (coarse_at < high_x)
+                coarse_line = jnp.where(inside, value, coarse_line)
+            lanes = slice(at * 128, (at + 1) * 128)
+            for part in range(SPACE // 8):
+                start = i * SPACE + part * 8
+                fine_weight[start : start + 8, lanes] = fine_line
+            for part in range(SPACE // 16):
+                start = i * (SPACE // 2) + part * 8
+                coarse_weight[start : start + 8, lanes] = coarse_line
 
     def rows_of(travel):
         if travel == 0:
@@ -862,9 +926,11 @@
         ref = mid if travel_x == 0 else (left_side if travel_x > 0 else right_side)
         return ref.at[:, rows_of(travel_y)[1]]
 
+    for load in loads:
+        load.wait()
     pl.semaphore_wait(barrier, greeters)
 
-    for index, (travel_y, travel_x) in enumerate(travels):
+    for index, (travel_y, travel_x) in sorted(enumerate(travels), key=lambda item: -abs(item[1][1])):
 
         @pl.when(exists(travel_y, travel_x))
         def _():
@@ -875,25 +941,31 @@
                 lanes = slice(breadth - 128, breadth)
             else:
                 lanes = slice(0, 128)
-            for image, ref in enumerate((fixed_hbm, moving_hbm)):
-                pltpu.make_async_remote_copy(
-                    src_ref=ref.at[source_rows, lanes],
-                    dst_ref=landing(travel_y, travel_x).at[image],
-                    send_sem=rim_send.at[index],
-                    recv_sem=rim_recv.at[index],
-                    device_id=(ty + travel_y, tx + travel_x),
-                    device_id_type=MESH,
-                ).start()
+            source_rows = slice(source_rows.start + RIM, source_rows.stop + RIM)
+            pltpu.make_async_remote_copy(
+                src_ref=mid.at[:, source_rows, lanes],
+                dst_ref=landing(travel_y, travel_x),
+                send_sem=rim_send.at[index],
+                recv_sem=rim_recv.at[index],
+                device_id=(ty + travel_y, tx + travel_x),
+                device_id_type=MESH,
+            ).start()
 
     if few:
         greet_far(ready)
-
-    knot = lax.broadcasted_iota(jnp.int32, (128, breadth), 0)
-    at_x = lax.broadcasted_iota(jnp.int32, (128, breadth), 1).astype(F32) / SPACE
-    last = bspline(at_x - (knot - tx * cells_x).astype(F32))
-    last_high, last_low = split(jnp.where(knot < knots_x, last, 0.0))
-    last_cols[:, :breadth] = last_high
-    last_cols[:, breadth:] = last_low
+    table_loads = []
+    for index, (source, target) in enumerate(zip(tables_hbm, tables)):
+        table_loads.append(pltpu.make_async_copy(source, target, table_sem.at[index]))
+        table_loads[index].start()
+
+    knot = lax.broadcasted_iota(jnp.int32, (128, 128), 0)
+    lane = lax.broadcasted_iota(jnp.int32, (128, 128), 1)
+    for at in range(PARTS):
+        at_x = (PARTS * lane + at - 8).astype(F32) / SPACE
+        last = bspline(at_x - (knot - tx * cells_x).astype(F32))
+        last_high, last_low = split(jnp.where(knot < knots_x, last, 0.0))
+        last_cols[:, at * 128 : (at + 1) * 128] = last_high
+        last_cols[:, wide + at * 128 : wide + (at + 1) * 128] = last_low
     knot = lax.broadcasted_iota(jnp.int32, (height, 128), 1)
     at_y = lax.broadcasted_iota(jnp.int32, (height, 128), 0).astype(F32) / SPACE
     third = knot // knots_y
@@ -903,9 +975,6 @@
     kept = jnp.where(third < 2, last_high.astype(F32), last_low.astype(F32))
     last_rows[...] = jnp.where(third < 3, kept, 0.0).astype(B16)
 
-    for load in loads:
-        load.wait()
-
     for index, (travel_y, travel_x) in enumerate(travels):
 
         @pl.when(exists(-travel_y, -travel_x))
@@ -928,52 +997,56 @@
             [full[base + tile, 8 : height + 24] for tile in range(tiles + 1)], axis=1
         )
 
-    def coarse_pair():
+    def coarse_image(image):
+        base = image * (tiles + 1)
         span = height // 2 + RIM
-        summed = []
-        for image in range(2):
-            base = image * (tiles + 1)
-            summed.append(
-                jnp.concatenate(
-                    [
-                        full[base + tile, pl.ds(0, span, stride=2), :]
-                        + full[base + tile, pl.ds(1, span, stride=2), :]
-                        for tile in range(tiles + 1)
-                    ],
-                    axis=1,
-                )
-            )
-        fixed, moving = summed
-        at = lax.broadcasted_iota(jnp.int32, fixed.shape, 1)
-        pair = jnp.where(
-            lax.rem(at, 2) == 0, fixed + moved(fixed, 0, 1), moving + moved(moving, 0, -1)
+        return jnp.concatenate(
+            [
+                full[base + tile, pl.ds(0, span, stride=2), :]
+                + full[base + tile, pl.ds(1, span, stride=2), :]
+                for tile in range(tiles + 1)
+            ],
+            axis=1,
         )
-        return 0.25 * pair
+
+    def parts_of(values):
+        return [values[:, at * 128 : (at + 1) * 128] for at in range(PARTS)]
 
     def coarse_terms_into():
-        pair = coarse_pair()
-        minds_tiled(minds_into(pair, 2, boxes_ref), boxes_ref, minds_ref, pair.shape[0])
+        pair = None
+        for image, table in enumerate((fixed_stride, moving_stride)):
+            pieces = split_three(coarse_image(image))
+            out = dot(jnp.concatenate(pieces, axis=0), table[...])
+            rows = pieces[0].shape[0]
+            out = out[:rows] + out[rows : 2 * rows] + out[2 * rows :]
+            pair = out if pair is None else pair + out
+        minds_tiled(boxes_into(parts_of(pair), boxes_ref), boxes_ref, minds_ref)
 
         def fixed_of(index, base, own):
-            return shifted_tiles(own, -1, tiles)
-
-        sums_into(minds_ref, fixed_of, 2, 2, coarse_terms)
+            return [pltpu.roll(part, 64, 1) for part in own]
+
+        sums_into(minds_ref, fixed_of, 2, coarse_terms)
 
     def fine_terms_into():
-        fixed_minds[...] = minds_into(fine_image(0), 1, fixed_boxes)[8 : 8 + height, :breadth]
-        image = fine_image(1)
-        minds_tiled(minds_into(image, 1, boxes_ref), boxes_ref, minds_ref, image.shape[0])
+        pieces = split_three(jnp.concatenate([fine_image(0), fine_image(1)], axis=0))
+        out = dot(jnp.concatenate(pieces, axis=0), fine_stride[...])
+        rows = height + 16
+        both = out[: 2 * rows] + out[2 * rows : 4 * rows] + out[4 * rows :]
+        scale = boxes_into(parts_of(both[:rows]), fixed_boxes)
+        for at in range(PARTS):
+            fixed_minds[:, at * 128 : (at + 1) * 128] = scale[at][8 : 8 + height]
+        minds_tiled(boxes_into(parts_of(both[rows:]), boxes_ref), boxes_ref, minds_ref)
 
         def fixed_of(index, base, own):
             return [
-                jnp.exp(
-                    fixed_boxes[index, base : base + 8, tile * 128 : (tile + 1) * 128]
-                    * fixed_minds[base - 8 : base, tile * 128 : (tile + 1) * 128]
+                jnp.exp2(
+                    fixed_boxes[index, at, base : base + 8]
+                    * fixed_minds[base - 8 : base, at * 128 : (at + 1) * 128]
                 )
-                for tile in range(tiles)
+                for at in range(PARTS)
             ]
 
-        sums_into(minds_ref, fixed_of, 1, 1, fine_terms)
+        sums_into(minds_ref, fixed_of, 1, fine_terms)
 
     def block_of(terms_ref, weight_ref, level):
         row_pairs, row_lines, col_table = level
@@ -992,15 +1065,15 @@
         return out[:BLOCK, :128] + out[BLOCK:, :128] + out[:BLOCK, 128:]
 
     def send_block(level, block):
-        boxes[level, parity, place] = block
+        boxes[level, parity, place, 0:used] = block[:used]
         order = [(a, b) for a in range(count_y) for b in range(count_x // 2) if a + b]
         for step_y, step_x in sorted(order, key=lambda p: abs(p[0] - count_y // 2) - p[1]):
             if True:
                 to_y = lax.rem(ty + step_y, count_y)
                 to_x = 2 * lax.rem(tx // 2 + step_x, count_x // 2) + parity
                 pltpu.make_async_remote_copy(
-                    src_ref=boxes.at[level, parity, place],
-                    dst_ref=boxes.at[level, parity, place],
+                    src_ref=boxes.at[level, parity, place, 0:used],
+                    dst_ref=boxes.at[level, parity, place, 0:used],
                     send_sem=block_send.at[level],
                     recv_sem=block_recv.at[level],
                     device_id=(to_y, to_x),
@@ -1009,37 +1082,36 @@
 
     def relay_of(level):
         return pltpu.make_async_remote_copy(
-            src_ref=boxes.at[level, parity],
-            dst_ref=boxes.at[level, parity],
+            src_ref=boxes.at[level, parity, :, 0:used],
+            dst_ref=boxes.at[level, parity, :, 0:used],
             send_sem=relay_send.at[level],
             recv_sem=relay_recv.at[level],
             device_id=sibling,
             device_id_type=MESH,
         )
 
+    def columns_of(level, side):
+        across = count_x // 2
+        columns = [
+            jnp.concatenate(
+                [boxes[level, side, to_y * across + to_x] for to_y in range(count_y)], axis=0
+            )
+            for to_x in range(across)
+        ]
+        upper, lower = split(jnp.concatenate(columns, axis=1))
+        lines = pl.ds(pl.multiple_of(side * (across * 128), 128), across * 128)
+        out = dot(jnp.concatenate([upper, lower], axis=0), gather_cols[lines])
+        return out[: count_y * BLOCK] + out[count_y * BLOCK :]
+
     def relay(level):
-        part = boxes.at[level, 0, 0 : half - 1]
+        part = boxes.at[level, 0, 0 : half - 1, 0:used]
         pltpu.make_async_copy(part, part, block_recv.at[level]).wait()
         relay_of(level).start()
-        spot = boxes.at[level, 1 - parity]
+
+    def assemble(level, own):
+        spot = boxes.at[level, 1 - parity, :, 0:used]
         pltpu.make_async_copy(spot, spot, relay_recv.at[level]).wait()
-
-    def assemble(level):
-        columns = []
-        for to_x in range(count_x):
-            columns.append(
-                jnp.concatenate(
-                    [
-                        boxes[level, to_x % 2, to_y * (count_x // 2) + to_x // 2]
-                        for to_y in range(count_y)
-                    ],
-                    axis=0,
-                )
-            )
-        upper, lower = split(jnp.concatenate(columns, axis=1))
-        out = dot(jnp.concatenate([upper, lower], axis=0), gather_cols[...])
-        rows = count_y * BLOCK
-        upper, lower = split(out[:rows] + out[rows:])
+        upper, lower = split(own + columns_of(level, 1 - parity))
         stencils[level] = dot(gather_rows[...], jnp.concatenate([upper, lower], axis=0))
 
     group = lax.broadcasted_iota(jnp.int32, (knots_y, 128), 1) // knots_x
@@ -1089,10 +1161,7 @@
         image = pull(level, gradient)
         step = inner(gradient, gradient) / inner(gradient, image)
         control = [c - step * g for c, g in zip(control, gradient)]
-        gradient = [g - step * i for g, i in zip(gradient, image)]
-        image = pull(level, gradient)
-        step = inner(gradient, gradient) / inner(gradient, image)
-        return [c - step * g for c, g in zip(control, gradient)]
+        return control, [g - step * i for g, i in zip(gradient, image)]
 
     for load in table_loads:
         load.wait()
@@ -1105,30 +1174,36 @@
     send_block(1, block_of(fine_terms, fine_weight, fine_tables))
 
     relay(0)
-    assemble(0)
+    assemble(0, columns_of(0, parity))
     control = [jnp.zeros((knots_y, 128), F32)] * 2
-    control = descend(0, control, start_of(0))
+    control, gradient = descend(0, control, start_of(0))
     relay(1)
-    assemble(1)
+    fine_own = columns_of(1, parity)
+    control, _ = descend(0, control, gradient)
+    assemble(1, fine_own)
     gradient = [b + i for b, i in zip(start_of(1), pull(1, control))]
-    control = descend(1, control, gradient)
+    control, gradient = descend(1, control, gradient)
+    control, _ = descend(1, control, gradient)
 
     upper, lower = split(jnp.concatenate(control, axis=0))
     rows = 2 * knots_y
     out = dot(jnp.concatenate([upper, lower], axis=0), last_cols[...])
-    lines = out[:rows, :breadth] + out[rows:, :breadth] + out[:rows, breadth:]
+    lines = out[:rows, :wide] + out[rows:, :wide] + out[:rows, wide:]
     upper, lower = split(jnp.concatenate([lines[:knots_y], lines[knots_y:]], axis=1))
-    blank = jnp.zeros((128 - 3 * knots_y, 2 * breadth), B16)
+    blank = jnp.zeros((128 - 3 * knots_y, 2 * wide), B16)
     field = dot(last_rows[...], jnp.concatenate([upper, lower, upper, blank], axis=0))
-    field_y, field_x = field[:, :breadth], field[:, breadth:]
+    field_y, field_x = field[:, :wide], field[:, wide:]
     pull_y = fine_terms[2] * field_y + fine_terms[3] * field_x
     pull_x = fine_terms[3] * field_y + fine_terms[4] * field_x
-    mismatch_ref[...] = (
+    mismatch = (
         fine_terms[5]
         + 2.0 * (fine_terms[0] * field_y + fine_terms[1] * field_x)
         + field_y * pull_y
         + field_x * pull_x
     )
+    upper, lower = split(mismatch)
+    out = dot(jnp.concatenate([upper, lower], axis=0), stride_back[...])
+    mismatch_ref[...] = out[:height] + out[height:]
     for member in range(2):
         own = pltpu.roll(control[member], lax.rem(128 - cells_x * tx, 128), 1)
         own = pltpu.roll(own, lax.rem(knots_y - cells_y * ty, knots_y), 0)
@@ -1142,7 +1217,7 @@
             pltpu.make_async_copy(spot, spot, rim_send.at[index]).wait()
 
     for level in range(2):
-        part = boxes.at[level, 0, 0 : half - 1]
+        part = boxes.at[level, 0, 0 : half - 1, 0:used]
         pltpu.make_async_copy(part, part, block_send.at[level]).wait()
         relay_of(level).wait_send()
 
@@ -1216,33 +1291,34 @@
     height, breadth = fixed_image.shape
     cells_y, cells_x = height // SPACE, breadth // SPACE
     count = count_y * count_x
-    tall, full_lanes = height + 2 * RIM, breadth + 128
+    tall, wide = height + 2 * RIM, PARTS * 128
     vmem, dma = pltpu.VMEM, pltpu.SemaphoreType.DMA
     tables = (
         level_tables(height, breadth, 1)
         + level_tables(height, breadth, 2)
         + assembly_tables(count_y, count_x, cells_y, cells_x)
+        + stride_tables(breadth)
     )
     scratch = [vmem(table.shape, B16) for table in tables] + [
         vmem((2, tall, breadth), F32),
         vmem((2, tall, 128), F32),
         vmem((2, tall, 128), F32),
         vmem((2 * (breadth // 128 + 1), tall, 128), F32),
-        vmem((12, height + 16, full_lanes), F32),
-        vmem((12, height + 16, full_lanes), F32),
-        vmem((12, breadth // 128 + 1, height + 16, 128), F32),
-        vmem((height, breadth), F32),
-        vmem((6, height, breadth), F32),
-        vmem((6, height // 2, breadth), F32),
-        vmem((height, breadth), F32),
-        vmem((height // 2, breadth), F32),
+        vmem((12, PARTS, height + 16, 128), F32),
+        vmem((12, PARTS, height + 16, 128), F32),
+        vmem((12, PARTS, height + 16, 128), F32),
+        vmem((height, wide), F32),
+        vmem((6, height, wide), F32),
+        vmem((6, height // 2, wide), F32),
+        vmem((height, wide), F32),
+        vmem((height // 2, wide), F32),
         pltpu.SMEM((cells_y, cells_x), jnp.int32),
         vmem((2, 2, count // 2, BLOCK, 128), F32),
         vmem((2, tables[7].shape[0], tables[6].shape[1]), F32),
         vmem((height, 128), B16),
-        vmem((128, 2 * breadth), B16),
+        vmem((128, 2 * wide), B16),
         dma((3,)),
-        dma((8,)),
+        dma((12,)),
         dma((8,)),
         dma((8,)),
         dma((2,)),
@@ -1260,7 +1336,7 @@
             jax.ShapeDtypeStruct((2, cells_y, cells_x), F32),
             jax.ShapeDtypeStruct((height, breadth), F32),
         ),
-        in_specs=[pl.BlockSpec(memory_space=pltpu.HBM)] * 11,
+        in_specs=[pl.BlockSpec(memory_space=pltpu.HBM)] * 15,
         out_specs=(
             pl.BlockSpec(memory_space=pltpu.VMEM),
             pl.BlockSpec(memory_space=pltpu.VMEM),

time: 24.3 us -> 22.5 us (0.926)
  Pallas kernels: 23.6 us -> 21.7 us
    pallas_call x1, Pallas kernels: 22.9 us -> 21.1 us  [gathered_call(): pl.pallas_call(functools.partial(gathered_kernel, count_y, count_x), out_...]
where the time goes in v4:
time: 22.5 us; the launch traced here: 22.3 us
  Pallas kernels  21.7 us (96%)
  between operations  0.64 us (3%)
    pallas_call x1, Pallas kernels, gathered_call(): pl.pallas_call(functools.partial(gathered_kernel, count_y, count_x), out_...  21.1 us
    pallas_call x1, Pallas kernels, shards(): pl.pallas_call(closing, out_shape=(jax.ShapeDtypeStruct(coef.shape, F32),...  0.65 us

profile of v4, /device:TPU:1, one launch (start us, length us, event | category | flops | bytes accessed | tf_op | source)
XLA Modules:
  0.0 22.3 jit_solution(14838060978305106408)
XLA Ops:
  0.6 21.1 %shard_map.158 = (f32[2,2,8]{2,1,0:T(2,128)S(1)}, f32[64,256]{1,0:T(8,128)S(1)}) custom-call(s32[2,8]{1,0:T(2,128)} %tissue_hbm.1, f32[64,256]{1,0:T(8,128)} %fixed_hbm.1, f32[64,256]{1,0:T(8,128)} %moving_hbm.1, bf16[16,192]{1,0:T(8,128)(2,1)} %constant.24.clone.rest_0_, bf16[16,384]{1,0:T(8,128)(2,1)} %constant.25.clone.rest_1_, ...), custom_call_target="tpu_custom_call" | custom-call | tf_op jit(solution)/shard_map/pallas_call | solution.py:1333
  21.7 0.7 %shard_map.159 = (f32[2,2,8]{2,1,0:T(2,128)}, f32[64,256]{1,0:T(8,128)}) custom-call(f32[2,2,8]{2,1,0:T(2,128)S(1)} %get-tuple-element.4.coef_in, f32[64,256]{1,0:T(8,128)S(1)} %get-tuple-element.5.mismatch_in), custom_call_target="tpu_custom_call" | custom-call | tf_op jit(solution)/shard_map/pallas_call | solution.py:1358

commit v5 on v4

--- a/solution.py
+++ b/solution.py
@@ -803,6 +803,7 @@
         stencils,
         last_rows,
         last_cols,
+        natural,
         load_sem,
         table_sem,
         rim_send,
@@ -958,14 +959,12 @@
         table_loads.append(pltpu.make_async_copy(source, target, table_sem.at[index]))
         table_loads[index].start()
 
-    knot = lax.broadcasted_iota(jnp.int32, (128, 128), 0)
-    lane = lax.broadcasted_iota(jnp.int32, (128, 128), 1)
-    for at in range(PARTS):
-        at_x = (PARTS * lane + at - 8).astype(F32) / SPACE
-        last = bspline(at_x - (knot - tx * cells_x).astype(F32))
-        last_high, last_low = split(jnp.where(knot < knots_x, last, 0.0))
-        last_cols[:, at * 128 : (at + 1) * 128] = last_high
-        last_cols[:, wide + at * 128 : wide + (at + 1) * 128] = last_low
+    knot = lax.broadcasted_iota(jnp.int32, (128, breadth), 0)
+    at_x = lax.broadcasted_iota(jnp.int32, (128, breadth), 1).astype(F32) / SPACE
+    last = bspline(at_x - (knot - tx * cells_x).astype(F32))
+    last_high, last_low = split(jnp.where(knot < knots_x, last, 0.0))
+    last_cols[:, :breadth] = last_high
+    last_cols[:, breadth:] = last_low
     knot = lax.broadcasted_iota(jnp.int32, (height, 128), 1)
     at_y = lax.broadcasted_iota(jnp.int32, (height, 128), 0).astype(F32) / SPACE
     third = knot // knots_y
@@ -1100,8 +1099,9 @@
         ]
         upper, lower = split(jnp.concatenate(columns, axis=1))
         lines = pl.ds(pl.multiple_of(side * (across * 128), 128), across * 128)
-        out = dot(jnp.concatenate([upper, lower], axis=0), gather_cols[lines])
-        return out[: count_y * BLOCK] + out[count_y * BLOCK :]
+        placed = dot(gather_rows[...], jnp.concatenate([upper, lower], axis=0))
+        out = dot(jnp.concatenate(split(placed), axis=0), gather_cols[lines])
+        return out[: placed.shape[0]] + out[placed.shape[0] :]
 
     def relay(level):
         part = boxes.at[level, 0, 0 : half - 1, 0:used]
@@ -1111,8 +1111,7 @@
     def assemble(level, own):
         spot = boxes.at[level, 1 - parity, :, 0:used]
         pltpu.make_async_copy(spot, spot, relay_recv.at[level]).wait()
-        upper, lower = split(own + columns_of(level, 1 - parity))
-        stencils[level] = dot(gather_rows[...], jnp.concatenate([upper, lower], axis=0))
+        stencils[level] = own + columns_of(level, 1 - parity)
 
     group = lax.broadcasted_iota(jnp.int32, (knots_y, 128), 1) // knots_x
 
@@ -1133,8 +1132,7 @@
             for member in range(2)
         ]
 
-    def pull(level, pair):
-        spreads = [spread(values) for values in pair]
+    def pull(level, spreads):
         sums = [None, None]
         for gap in range(-3, 4):
             at = (gap + 3) * knots_y
@@ -1158,7 +1156,7 @@
         return jnp.sum(first[0] * second[0] + first[1] * second[1], keepdims=True)
 
     def descend(level, control, gradient):
-        image = pull(level, gradient)
+        image = pull(level, [spread(values) for values in gradient])
         step = inner(gradient, gradient) / inner(gradient, image)
         control = [c - step * g for c, g in zip(control, gradient)]
         return control, [g - step * i for g, i in zip(gradient, image)]
@@ -1173,6 +1171,11 @@
     fine_terms_into()
     send_block(1, block_of(fine_terms, fine_weight, fine_tables))
 
+    for term in range(6):
+        pieces = split_three(fine_terms[term])
+        out = dot(jnp.concatenate(pieces, axis=0), stride_back[...])
+        natural[term] = out[:height] + out[height : 2 * height] + out[2 * height :]
+
     relay(0)
     assemble(0, columns_of(0, parity))
     control = [jnp.zeros((knots_y, 128), F32)] * 2
@@ -1180,30 +1183,28 @@
     relay(1)
     fine_own = columns_of(1, parity)
     control, _ = descend(0, control, gradient)
+    spreads = [spread(values) for values in control]
     assemble(1, fine_own)
-    gradient = [b + i for b, i in zip(start_of(1), pull(1, control))]
+    gradient = [b + i for b, i in zip(start_of(1), pull(1, spreads))]
     control, gradient = descend(1, control, gradient)
     control, _ = descend(1, control, gradient)
 
     upper, lower = split(jnp.concatenate(control, axis=0))
     rows = 2 * knots_y
     out = dot(jnp.concatenate([upper, lower], axis=0), last_cols[...])
-    lines = out[:rows, :wide] + out[rows:, :wide] + out[:rows, wide:]
+    lines = out[:rows, :breadth] + out[rows:, :breadth] + out[:rows, breadth:]
     upper, lower = split(jnp.concatenate([lines[:knots_y], lines[knots_y:]], axis=1))
-    blank = jnp.zeros((128 - 3 * knots_y, 2 * wide), B16)
+    blank = jnp.zeros((128 - 3 * knots_y, 2 * breadth), B16)
     field = dot(last_rows[...], jnp.concatenate([upper, lower, upper, blank], axis=0))
-    field_y, field_x = field[:, :wide], field[:, wide:]
-    pull_y = fine_terms[2] * field_y + fine_terms[3] * field_x
-    pull_x = fine_terms[3] * field_y + fine_terms[4] * field_x
-    mismatch = (
-        fine_terms[5]
-        + 2.0 * (fine_terms[0] * field_y + fine_terms[1] * field_x)
+    field_y, field_x = field[:, :breadth], field[:, breadth:]
+    pull_y = natural[2] * field_y + natural[3] * field_x
+    pull_x = natural[3] * field_y + natural[4] * field_x
+    mismatch_ref[...] = (
+        natural[5]
+        + 2.0 * (natural[0] * field_y + natural[1] * field_x)
         + field_y * pull_y
         + field_x * pull_x
     )
-    upper, lower = split(mismatch)
-    out = dot(jnp.concatenate([upper, lower], axis=0), stride_back[...])
-    mismatch_ref[...] = out[:height] + out[height:]
     for member in range(2):
         own = pltpu.roll(control[member], lax.rem(128 - cells_x * tx, 128), 1)
         own = pltpu.roll(own, lax.rem(knots_y - cells_y * ty, knots_y), 0)
@@ -1316,7 +1317,8 @@
         vmem((2, 2, count // 2, BLOCK, 128), F32),
         vmem((2, tables[7].shape[0], tables[6].shape[1]), F32),
         vmem((height, 128), B16),
-        vmem((128, 2 * wide), B16),
+        vmem((128, 2 * breadth), B16),
+        vmem((6, height, breadth), F32),
         dma((3,)),
         dma((12,)),
         dma((8,)),

time: 22.5 us -> 22.2 us (0.987)
  Pallas kernels: 21.7 us -> 21.4 us
    pallas_call x1, Pallas kernels: 21.1 us -> 20.7 us  [gathered_call(): pl.pallas_call(functools.partial(gathered_kernel, count_y, count_x), out_...]
where the time goes in v5:
time: 22.2 us; the launch traced here: 22 us
  Pallas kernels  21.4 us (96%)
  between operations  0.64 us (3%)
    pallas_call x1, Pallas kernels, gathered_call(): pl.pallas_call(functools.partial(gathered_kernel, count_y, count_x), out_...  20.7 us
    pallas_call x1, Pallas kernels, shards(): pl.pallas_call(closing, out_shape=(jax.ShapeDtypeStruct(coef.shape, F32),...  0.65 us

profile of v5, /device:TPU:1, one launch (start us, length us, event | category | flops | bytes accessed | tf_op | source)
XLA Modules:
  0.0 22.0 jit_solution(13706445587288354281)
XLA Ops:
  0.6 20.7 %shard_map.158 = (f32[2,2,8]{2,1,0:T(2,128)S(1)}, f32[64,256]{1,0:T(8,128)S(1)}) custom-call(s32[2,8]{1,0:T(2,128)} %tissue_hbm.1, f32[64,256]{1,0:T(8,128)} %fixed_hbm.1, f32[64,256]{1,0:T(8,128)} %moving_hbm.1, bf16[16,192]{1,0:T(8,128)(2,1)} %constant.24.clone.rest_0_, bf16[16,384]{1,0:T(8,128)(2,1)} %constant.25.clone.rest_1_, ...), custom_call_target="tpu_custom_call" | custom-call | tf_op jit(solution)/shard_map/pallas_call | solution.py:1335
  21.4 0.7 %shard_map.159 = (f32[2,2,8]{2,1,0:T(2,128)}, f32[64,256]{1,0:T(8,128)}) custom-call(f32[2,2,8]{2,1,0:T(2,128)S(1)} %get-tuple-element.4.coef_in, f32[64,256]{1,0:T(8,128)S(1)} %get-tuple-element.5.mismatch_in), custom_call_target="tpu_custom_call" | custom-call | tf_op jit(solution)/shard_map/pallas_call | solution.py:1360

commit v6 on v5

--- a/solution.py
+++ b/solution.py
@@ -598,7 +598,7 @@
             for side in range(2):
                 coarse[image, natural_lane(2 * (place - 6) + side, breadth), at] = 0.25
     back = fine[:breadth].T
-    return tuple(table.astype(B16) for table in (fine, coarse[0], coarse[1], back))
+    return tuple(table.astype(B16) for table in (fine, coarse.reshape(-1, PARTS * 128), back))
 
 
 def level_tables(height, breadth, factor):
@@ -782,9 +782,9 @@
     moving_hbm,
     *rest,
 ):
-    tables_hbm, rest = rest[:12], rest[12:]
+    tables_hbm, rest = rest[:11], rest[11:]
     coef_ref, mismatch_ref = rest[:2]
-    tables, rest = rest[2:14], rest[14:]
+    tables, rest = rest[2:13], rest[13:]
     (
         mid,
         left_side,
@@ -815,7 +815,7 @@
         ready,
     ) = rest
     fine_tables, coarse_tables, (gather_cols, gather_rows) = tables[:3], tables[3:6], tables[6:8]
-    fine_stride, fixed_stride, moving_stride, stride_back = tables[8:]
+    fine_stride, coarse_stride, stride_back = tables[8:]
     ty = lax.axis_index("ty")
     tx = lax.axis_index("tx")
     count = count_y * count_x
@@ -1012,13 +1012,10 @@
         return [values[:, at * 128 : (at + 1) * 128] for at in range(PARTS)]
 
     def coarse_terms_into():
-        pair = None
-        for image, table in enumerate((fixed_stride, moving_stride)):
-            pieces = split_three(coarse_image(image))
-            out = dot(jnp.concatenate(pieces, axis=0), table[...])
-            rows = pieces[0].shape[0]
-            out = out[:rows] + out[rows : 2 * rows] + out[2 * rows :]
-            pair = out if pair is None else pair + out
+        pieces = split_three(jnp.concatenate([coarse_image(0), coarse_image(1)], axis=1))
+        out = dot(jnp.concatenate(pieces, axis=0), coarse_stride[...])
+        rows = pieces[0].shape[0]
+        pair = out[:rows] + out[rows : 2 * rows] + out[2 * rows :]
         minds_tiled(boxes_into(parts_of(pair), boxes_ref), boxes_ref, minds_ref)
 
         def fixed_of(index, base, own):
@@ -1065,9 +1062,10 @@
 
     def send_block(level, block):
         boxes[level, parity, place, 0:used] = block[:used]
-        order = [(a, b) for a in range(count_y) for b in range(count_x // 2) if a + b]
-        for step_y, step_x in sorted(order, key=lambda p: abs(p[0] - count_y // 2) - p[1]):
-            if True:
+        for step_y in [*range(1, count_y), 0]:
+            for step_x in reversed(range(count_x // 2)):
+                if step_y + step_x == 0:
+                    continue
                 to_y = lax.rem(ty + step_y, count_y)
                 to_x = 2 * lax.rem(tx // 2 + step_x, count_x // 2) + parity
                 pltpu.make_async_remote_copy(
@@ -1338,7 +1336,7 @@
             jax.ShapeDtypeStruct((2, cells_y, cells_x), F32),
             jax.ShapeDtypeStruct((height, breadth), F32),
         ),
-        in_specs=[pl.BlockSpec(memory_space=pltpu.HBM)] * 15,
+        in_specs=[pl.BlockSpec(memory_space=pltpu.HBM)] * 14,
         out_specs=(
             pl.BlockSpec(memory_space=pltpu.VMEM),
             pl.BlockSpec(memory_space=pltpu.VMEM),

time: 22.2 us -> 21.9 us (0.986)
  Pallas kernels: 21.4 us -> 21.1 us
    pallas_call x1, Pallas kernels: 20.7 us -> 20.4 us  [gathered_call(): pl.pallas_call(functools.partial(gathered_kernel, count_y, count_x), out_...]
where the time goes in v6:
time: 21.9 us; the launch traced here: 21.7 us
  Pallas kernels  21.1 us (96%)
  between operations  0.64 us (3%)
    pallas_call x1, Pallas kernels, gathered_call(): pl.pallas_call(functools.partial(gathered_kernel, count_y, count_x), out_...  20.4 us
    pallas_call x1, Pallas kernels, shards(): pl.pallas_call(closing, out_shape=(jax.ShapeDtypeStruct(coef.shape, F32),...  0.65 us

profile of v6, /device:TPU:1, one launch (start us, length us, event | category | flops | bytes accessed | tf_op | source)
XLA Modules:
  0.0 21.7 jit_solution(14870778314823604961)
XLA Ops:
  0.6 20.4 %shard_map.149 = (f32[2,2,8]{2,1,0:T(2,128)S(1)}, f32[64,256]{1,0:T(8,128)S(1)}) custom-call(s32[2,8]{1,0:T(2,128)} %tissue_hbm.1, f32[64,256]{1,0:T(8,128)} %fixed_hbm.1, f32[64,256]{1,0:T(8,128)} %moving_hbm.1, bf16[16,192]{1,0:T(8,128)(2,1)} %constant.22.clone.rest_0_, bf16[16,384]{1,0:T(8,128)(2,1)} %constant.23.clone.rest_1_, ...), custom_call_target="tpu_custom_call" | custom-call | tf_op jit(solution)/shard_map/pallas_call | solution.py:1333
  21.0 0.7 %shard_map.150 = (f32[2,2,8]{2,1,0:T(2,128)}, f32[64,256]{1,0:T(8,128)}) custom-call(f32[2,2,8]{2,1,0:T(2,128)S(1)} %get-tuple-element.4.coef_in, f32[64,256]{1,0:T(8,128)S(1)} %get-tuple-element.5.mismatch_in), custom_call_target="tpu_custom_call" | custom-call | tf_op jit(solution)/shard_map/pallas_call | solution.py:1358

commit v7 on v6

--- a/solution.py
+++ b/solution.py
@@ -872,7 +872,6 @@
         )
         loads[image].start()
 
-    boxes[:, :, :, used:] = jnp.zeros((2, 2, half, BLOCK - used, 128), F32)
     low, high = slice(0, RIM), slice(RIM + height, 2 * RIM + height)
 
     @pl.when(ty == 0)
@@ -893,6 +892,50 @@
     def _():
         right_side[...] = jnp.zeros(right_side.shape, F32)
 
+    def rows_of(travel):
+        if travel == 0:
+            return slice(0, height), slice(RIM, RIM + height)
+        if travel > 0:
+            return slice(height - RIM, height), low
+        return slice(0, RIM), high
+
+    def landing(travel_y, travel_x):
+        ref = mid if travel_x == 0 else (left_side if travel_x > 0 else right_side)
+        return ref.at[:, rows_of(travel_y)[1]]
+
+    for load in loads:
+        load.wait()
+    pl.semaphore_wait(barrier, greeters)
+
+    for index, (travel_y, travel_x) in sorted(enumerate(travels), key=lambda item: -abs(item[1][1])):
+
+        @pl.when(exists(travel_y, travel_x))
+        def _():
+            source_rows = rows_of(travel_y)[0]
+            if travel_x == 0:
+                lanes = slice(0, breadth)
+            elif travel_x > 0:
+                lanes = slice(breadth - 128, breadth)
+            else:
+                lanes = slice(0, 128)
+            source_rows = slice(source_rows.start + RIM, source_rows.stop + RIM)
+            pltpu.make_async_remote_copy(
+                src_ref=mid.at[:, source_rows, lanes],
+                dst_ref=landing(travel_y, travel_x),
+                send_sem=rim_send.at[index],
+                recv_sem=rim_recv.at[index],
+                device_id=(ty + travel_y, tx + travel_x),
+                device_id_type=MESH,
+            ).start()
+
+    if few:
+        greet_far(ready)
+    table_loads = []
+    for index, (source, target) in enumerate(zip(tables_hbm, tables)):
+        table_loads.append(pltpu.make_async_copy(source, target, table_sem.at[index]))
+        table_loads[index].start()
+
+    boxes[:, :, :, used:] = jnp.zeros((2, 2, half, BLOCK - used, 128), F32)
     lane = lax.broadcasted_iota(jnp.int32, (8, 128), 1)
     tissue_load.wait()
     for i in range(cells_y):
@@ -916,49 +959,6 @@
                 start = i * (SPACE // 2) + part * 8
                 coarse_weight[start : start + 8, lanes] = coarse_line
 
-    def rows_of(travel):
-        if travel == 0:
-            return slice(0, height), slice(RIM, RIM + height)
-        if travel > 0:
-            return slice(height - RIM, height), low
-        return slice(0, RIM), high
-
-    def landing(travel_y, travel_x):
-        ref = mid if travel_x == 0 else (left_side if travel_x > 0 else right_side)
-        return ref.at[:, rows_of(travel_y)[1]]
-
-    for load in loads:
-        load.wait()
-    pl.semaphore_wait(barrier, greeters)
-
-    for index, (travel_y, travel_x) in sorted(enumerate(travels), key=lambda item: -abs(item[1][1])):
-
-        @pl.when(exists(travel_y, travel_x))
-        def _():
-            source_rows = rows_of(travel_y)[0]
-            if travel_x == 0:
-                lanes = slice(0, breadth)
-            elif travel_x > 0:
-                lanes = slice(breadth - 128, breadth)
-            else:
-                lanes = slice(0, 128)
-            source_rows = slice(source_rows.start + RIM, source_rows.stop + RIM)
-            pltpu.make_async_remote_copy(
-                src_ref=mid.at[:, source_rows, lanes],
-                dst_ref=landing(travel_y, travel_x),
-                send_sem=rim_send.at[index],
-                recv_sem=rim_recv.at[index],
-                device_id=(ty + travel_y, tx + travel_x),
-                device_id_type=MESH,
-            ).start()
-
-    if few:
-        greet_far(ready)
-    table_loads = []
-    for index, (source, target) in enumerate(zip(tables_hbm, tables)):
-        table_loads.append(pltpu.make_async_copy(source, target, table_sem.at[index]))
-        table_loads[index].start()
-
     knot = lax.broadcasted_iota(jnp.int32, (128, breadth), 0)
     at_x = lax.broadcasted_iota(jnp.int32, (128, breadth), 1).astype(F32) / SPACE
     last = bspline(at_x - (knot - tx * cells_x).astype(F32))
@@ -1024,14 +1024,16 @@
         sums_into(minds_ref, fixed_of, 2, coarse_terms)
 
     def fine_terms_into():
-        pieces = split_three(jnp.concatenate([fine_image(0), fine_image(1)], axis=0))
-        out = dot(jnp.concatenate(pieces, axis=0), fine_stride[...])
         rows = height + 16
-        both = out[: 2 * rows] + out[2 * rows : 4 * rows] + out[4 * rows :]
-        scale = boxes_into(parts_of(both[:rows]), fixed_boxes)
+        turned = []
+        for image in range(2):
+            pieces = split_three(fine_image(image))
+            out = dot(jnp.concatenate(pieces, axis=0), fine_stride[...])
+            turned.append(parts_of(out[:rows] + out[rows : 2 * rows] + out[2 * rows :]))
+        scale = boxes_into(turned[0], fixed_boxes)
         for at in range(PARTS):
             fixed_minds[:, at * 128 : (at + 1) * 128] = scale[at][8 : 8 + height]
-        minds_tiled(boxes_into(parts_of(both[rows:]), boxes_ref), boxes_ref, minds_ref)
+        minds_tiled(boxes_into(turned[1], boxes_ref), boxes_ref, minds_ref)
 
         def fixed_of(index, base, own):
             return [

time: 21.9 us -> 21.7 us (level)
  no operation moved by 1% of the time
where the time goes in v7:
time: 21.7 us; the launch traced here: 21.6 us
  Pallas kernels  20.9 us (96%)
  between operations  0.64 us (3%)
    pallas_call x1, Pallas kernels, gathered_call(): pl.pallas_call(functools.partial(gathered_kernel, count_y, count_x), out_...  20.3 us
    pallas_call x1, Pallas kernels, shards(): pl.pallas_call(closing, out_shape=(jax.ShapeDtypeStruct(coef.shape, F32),...  0.65 us

profile of v7, /device:TPU:1, one launch (start us, length us, event | category | flops | bytes accessed | tf_op | source)
XLA Modules:
  0.0 21.6 jit_solution(14158646262249498778)
XLA Ops:
  0.6 20.3 %shard_map.149 = (f32[2,2,8]{2,1,0:T(2,128)S(1)}, f32[64,256]{1,0:T(8,128)S(1)}) custom-call(s32[2,8]{1,0:T(2,128)} %tissue_hbm.1, f32[64,256]{1,0:T(8,128)} %fixed_hbm.1, f32[64,256]{1,0:T(8,128)} %moving_hbm.1, bf16[16,192]{1,0:T(8,128)(2,1)} %constant.22.clone.rest_0_, bf16[16,384]{1,0:T(8,128)(2,1)} %constant.23.clone.rest_1_, ...), custom_call_target="tpu_custom_call" | custom-call | tf_op jit(solution)/shard_map/pallas_call | solution.py:1335
  20.9 0.7 %shard_map.150 = (f32[2,2,8]{2,1,0:T(2,128)}, f32[64,256]{1,0:T(8,128)}) custom-call(f32[2,2,8]{2,1,0:T(2,128)S(1)} %get-tuple-element.4.coef_in, f32[64,256]{1,0:T(8,128)S(1)} %get-tuple-element.5.mismatch_in), custom_call_target="tpu_custom_call" | custom-call | tf_op jit(solution)/shard_map/pallas_call | solution.py:1360

commit v8 on v7

--- a/solution.py
+++ b/solution.py
@@ -930,9 +930,12 @@
 
     if few:
         greet_far(ready)
-    table_loads = []
-    for index, (source, target) in enumerate(zip(tables_hbm, tables)):
-        table_loads.append(pltpu.make_async_copy(source, target, table_sem.at[index]))
+    table_loads = [
+        pltpu.make_async_copy(source, target, table_sem.at[index])
+        for index, (source, target) in enumerate(zip(tables_hbm, tables))
+    ]
+    early, late = (9, 3, 4, 5), (8, 0, 1, 2, 6, 7, 10)
+    for index in early + late:
         table_loads[index].start()
 
     boxes[:, :, :, used:] = jnp.zeros((2, 2, half, BLOCK - used, 128), F32)
@@ -1161,13 +1164,15 @@
         control = [c - step * g for c, g in zip(control, gradient)]
         return control, [g - step * i for g, i in zip(gradient, image)]
 
-    for load in table_loads:
-        load.wait()
+    for index in early:
+        table_loads[index].wait()
     coarse_terms_into()
     coarse_block = block_of(coarse_terms, coarse_weight, coarse_tables)
     if few:
         pl.semaphore_wait(ready, len(far_greets))
     send_block(0, coarse_block)
+    for index in late:
+        table_loads[index].wait()
     fine_terms_into()
     send_block(1, block_of(fine_terms, fine_weight, fine_tables))
 

time: 21.7 us -> 21.7 us (level)
  no operation moved by 1% of the time
where the time goes in v8:
time: 21.7 us; the launch traced here: 21.5 us
  Pallas kernels  20.9 us (96%)
  between operations  0.64 us (3%)
    pallas_call x1, Pallas kernels, gathered_call(): pl.pallas_call(functools.partial(gathered_kernel, count_y, count_x), out_...  20.3 us
    pallas_call x1, Pallas kernels, shards(): pl.pallas_call(closing, out_shape=(jax.ShapeDtypeStruct(coef.shape, F32),...  0.65 us

profile of v8, /device:TPU:1, one launch (start us, length us, event | category | flops | bytes accessed | tf_op | source)
XLA Modules:
  0.0 21.5 jit_solution(17464240354416562135)
XLA Ops:
  0.6 20.3 %shard_map.149 = (f32[2,2,8]{2,1,0:T(2,128)S(1)}, f32[64,256]{1,0:T(8,128)S(1)}) custom-call(s32[2,8]{1,0:T(2,128)} %tissue_hbm.1, f32[64,256]{1,0:T(8,128)} %fixed_hbm.1, f32[64,256]{1,0:T(8,128)} %moving_hbm.1, bf16[16,192]{1,0:T(8,128)(2,1)} %constant.22.clone.rest_0_, bf16[16,384]{1,0:T(8,128)(2,1)} %constant.23.clone.rest_1_, ...), custom_call_target="tpu_custom_call" | custom-call | tf_op jit(solution)/shard_map/pallas_call | solution.py:1340
  20.9 0.7 %shard_map.150 = (f32[2,2,8]{2,1,0:T(2,128)}, f32[64,256]{1,0:T(8,128)}) custom-call(f32[2,2,8]{2,1,0:T(2,128)S(1)} %get-tuple-element.4.coef_in, f32[64,256]{1,0:T(8,128)S(1)} %get-tuple-element.5.mismatch_in), custom_call_target="tpu_custom_call" | custom-call | tf_op jit(solution)/shard_map/pallas_call | solution.py:1365
